TPU v7x, 32 devices: a whole 2x2x4 slice. The times are simulated.
32 devices in a mesh: dp: 4 (over y, x), ctx: 8 (over z, core).
Axes of the slice: x: 2, y: 2, z: 4, core: 2. Of those that a mesh axis runs over, the one named last changes fastest.
Arguments:
- query: bfloat16 [4, 1024, 4096], P('dp', 'ctx'), may hold values from -5 to 5
- keys: bfloat16 [4, 1024, 512], P('dp', 'ctx'), may hold values from -5 to 5
- values: bfloat16 [4, 1024, 512], P('dp', 'ctx'), may hold values from -6 to 6
- out_grad: bfloat16 [4, 1024, 4096], P('dp', 'ctx'), may hold values from -16 to 16
- query_lowrank_state: bfloat16 [4, 1024, 8], P('dp', 'ctx'), may hold values from -0.25 to 0.25
- value_lowrank_state: bfloat16 [4, 1024, 8], P('dp', 'ctx'), may hold values from -0.25 to 0.25
- shift_flags: int32 [4], replicated, may hold values from 0 to 1, as said below
Outputs:
- query_gradient: bfloat16 [4, 1024, 4096], P('dp', 'ctx')
- key_gradient: bfloat16 [4, 1024, 512], P('dp', 'ctx')
- value_gradient: bfloat16 [4, 1024, 512], P('dp', 'ctx')
- query_adapter_gradient: float32 [8, 4096], replicated
- value_adapter_gradient: float32 [8, 512], replicated
Inputs may be any that keep to these rules, and one draw needn't show every extreme that they name: `shift_flags`: exactly half of the 4 entries are 1, the others 0.
All inputs are finite; a program needn't handle non-finite values.
Results may differ from a plain program's by a relative error of at most 0.012.
Values may be sent and summed in bfloat16 or wider, within the bound.
A program may use at most 64 MiB of HBM per device.

v0:
```python
import functools
import math

import jax
import jax.numpy as jnp
from jax import lax
from jax.experimental import pallas as pl
from jax.experimental.pallas import tpu as pltpu
from jax.sharding import PartitionSpec as P

KV_HEADS = 4
PER_GROUP = 8
WIDTH = 128
TOK = 128
GROUP_CHIPS = 4
SPAN = PER_GROUP * WIDTH
ADAPTER_SCALE = 2.0
SCORE_SCALE = 1.0 / math.sqrt(WIDTH)
EXP2_SCALE = SCORE_SCALE * math.log2(math.e)
MESH = pl.DeviceIdType.MESH
F32 = jnp.float32
BF16 = jnp.bfloat16


def arrange_kernel(order, q, d, k, v, q_out, d_out, kv_out):
    q_out[0] = q[...]
    d_out[0] = d[...]
    kv_out[0, 0] = k[...]
    kv_out[0, 1] = v[...]


def arrange(order, q, d, k, v):
    spec = pltpu.PrefetchScalarGridSpec(
        num_scalar_prefetch=1,
        grid=(KV_HEADS,),
        in_specs=[
            pl.BlockSpec((TOK, SPAN), lambda s, o: (0, o[s])),
            pl.BlockSpec((TOK, SPAN), lambda s, o: (0, o[s])),
            pl.BlockSpec((TOK, WIDTH), lambda s, o: (0, o[s])),
            pl.BlockSpec((TOK, WIDTH), lambda s, o: (0, o[s])),
        ],
        out_specs=[
            pl.BlockSpec((1, TOK, SPAN), lambda s, o: (s, 0, 0)),
            pl.BlockSpec((1, TOK, SPAN), lambda s, o: (s, 0, 0)),
            pl.BlockSpec((1, 2, TOK, WIDTH), lambda s, o: (s, 0, 0, 0)),
        ],
    )
    return pl.pallas_call(
        arrange_kernel,
        grid_spec=spec,
        out_shape=[
            jax.ShapeDtypeStruct((KV_HEADS, TOK, SPAN), BF16),
            jax.ShapeDtypeStruct((KV_HEADS, TOK, SPAN), BF16),
            jax.ShapeDtypeStruct((KV_HEADS, 2, TOK, WIDTH), BF16),
        ],
        name="arrange_heads",
    )(order, q, d, k, v)


def restore_kernel(place, q, k, v, qa, va, q_out, k_out, v_out, qa_out, va_out):
    q_out[...] = q[0]
    k_out[...] = k[0]
    v_out[...] = v[0]
    qa_out[...] = qa[...]
    va_out[...] = va[...]


def restore(place, q, k, v, qa, va):
    wide = pl.BlockSpec((1, TOK, SPAN), lambda h, p: (p[h], 0, 0))
    narrow = pl.BlockSpec((1, TOK, WIDTH), lambda h, p: (p[h], 0, 0))
    spec = pltpu.PrefetchScalarGridSpec(
        num_scalar_prefetch=1,
        grid=(KV_HEADS,),
        in_specs=[
            wide,
            narrow,
            narrow,
            pl.BlockSpec((8, SPAN), lambda h, p: (0, p[h])),
            pl.BlockSpec((8, WIDTH), lambda h, p: (0, p[h])),
        ],
        out_specs=[
            pl.BlockSpec((TOK, SPAN), lambda h, p: (0, h)),
            pl.BlockSpec((TOK, WIDTH), lambda h, p: (0, h)),
            pl.BlockSpec((TOK, WIDTH), lambda h, p: (0, h)),
            pl.BlockSpec((8, SPAN), lambda h, p: (0, h)),
            pl.BlockSpec((8, WIDTH), lambda h, p: (0, h)),
        ],
    )
    return pl.pallas_call(
        restore_kernel,
        grid_spec=spec,
        out_shape=[
            jax.ShapeDtypeStruct((TOK, KV_HEADS * SPAN), BF16),
            jax.ShapeDtypeStruct((TOK, KV_HEADS * WIDTH), BF16),
            jax.ShapeDtypeStruct((TOK, KV_HEADS * WIDTH), BF16),
            jax.ShapeDtypeStruct((8, KV_HEADS * SPAN), F32),
            jax.ShapeDtypeStruct((8, KV_HEADS * WIDTH), F32),
        ],
        name="restore_heads",
    )(place, q, k, v, qa, va)


def dot(a, b, dims):
    return lax.dot_general(a, b, (dims, ((), ())), preferred_element_type=F32)


NT = ((1,), (1,))
NN = ((1,), (0,))


def attend(nb, us, pair, core_unused, qb, db, kvb, kT, cosT, sinT, acc, dqb):
    cols = [pl.ds(pl.multiple_of(pair * 2 * WIDTH + g * WIDTH, WIDTH), WIDTH) for g in range(2)]
    rows_q = jnp.concatenate([qb[us, h, :, cols[g]] for g in range(2) for h in range(2)], axis=0)
    rows_d = jnp.concatenate([db[us, h, :, cols[g]] for g in range(2) for h in range(2)], axis=0)
    n_rows = 4 * TOK
    score = []
    dprob = []
    for t in range(nb):
        key = kvb[us, t, :, 0].reshape(2 * TOK, WIDTH)
        val = kvb[us, t, :, 1].reshape(2 * TOK, WIDTH)
        s = dot(key, rows_q, NT)
        if t == 0:
            kpos = lax.broadcasted_iota(jnp.int32, (2 * TOK, n_rows), 0)
            rpos = lax.broadcasted_iota(jnp.int32, (2 * TOK, n_rows), 1) & (2 * TOK - 1)
            s = jnp.where(kpos <= rpos, s, -jnp.inf)
        score.append(s)
        dprob.append(dot(val, rows_d, NT))
    top = functools.reduce(jnp.maximum, [jnp.max(s, axis=0, keepdims=True) for s in score])
    weight = [jnp.exp2((s - top) * EXP2_SCALE) for s in score]
    total = sum(jnp.sum(w, axis=0, keepdims=True) for w in weight)
    mixed = sum(jnp.sum(w * dp, axis=0, keepdims=True) for w, dp in zip(weight, dprob))
    inverse = 1.0 / total
    delta = mixed * inverse
    dqT = jnp.zeros((WIDTH, n_rows), F32)
    for t in range(nb):
        prob = weight[t] * inverse
        ds = (prob * (dprob[t] - delta)).astype(BF16)
        acc[t, 1] += dot(prob.astype(BF16), rows_d, NN)
        acc[t, 0] += dot(ds, rows_q, NN)
        dqT = dqT + dot(kT[t], ds, NN)
    cos = cosT[...]
    sin = sinT[...]
    cos = jnp.concatenate([cos, cos], axis=1)
    sin = jnp.concatenate([sin, sin], axis=1)
    front = dqT[: WIDTH // 2] * SCORE_SCALE
    back = dqT[WIDTH // 2 :] * SCORE_SCALE
    turned = jnp.concatenate([front * cos + back * sin, back * cos - front * sin], axis=0)
    dq = turned.T.astype(BF16)
    for g in range(2):
        for h in range(2):
            at = (g * 2 + h) * TOK
            dqb[us, h, :, cols[g]] = dq[at : at + TOK]


def main_kernel(
    n, ndp,
    q, d, kv, st, cosT, sinT, cosF, sinF,
    qg, kg, vg, qa, va,
    qb, db, kvb, stb, kT, acc, psend, rbuf, dqb, own,
    qap, qzr, qds, qdr, qas, vap, vzr, vds, vdr,
    kvs, kvr, qs, qr, ss, sr, ps, pr, dqs, dqr,
    qzs_s, qzr_s, qds_s, qdr_s, qas_s, qar_s, vzs_s, vzr_s, vds_s, vdr_s,
):
    nz = n // 2
    wide = 2 * SPAN // nz
    me = lax.axis_index("ctx")
    dpi = lax.axis_index("dp")
    z = me // 2
    c = me % 2
    other = 1 - c
    sib = z * 2 + other

    def slot(us, zz):
        return (zz + 2 * us) % GROUP_CHIPS

    def copy(src, dst, send, recv, target):
        return pltpu.make_async_remote_copy(
            src_ref=src, dst_ref=dst, send_sem=send, recv_sem=recv,
            device_id=target, device_id_type=MESH,
        )

    barrier = pltpu.get_barrier_semaphore()

    @pl.loop(1, n)
    def _(o):
        pl.semaphore_signal(barrier, inc=1, device_id=(dpi, (me + o) % n), device_id_type=MESH)

    @pl.loop(1, ndp)
    def _(o):
        pl.semaphore_signal(barrier, inc=1, device_id=((dpi + o) % ndp, me), device_id_type=MESH)

    pl.semaphore_wait(barrier, n - 1 + ndp - 1)

    def near_kv(us):
        return copy(kv.at[2 * other + us], kvb.at[us, 0, c], kvs.at[us, 0, other], kvr.at[us, 0, c], (dpi, sib))

    def far_kv(us, t, cc):
        zt = (z + t) % nz
        return copy(kv.at[2 * cc + us], kvb.at[us, t, c], kvs.at[us, t, cc], kvr.at[us, t, c], (dpi, 2 * zt + cc))

    def near_rows(us, i):
        src, dst = ((q, qb), (d, db))[i]
        return copy(src.at[2 * other + us], dst.at[us, c], qs.at[us, i], qr.at[us, i], (dpi, sib))

    def near_state():
        return copy(st, stb.at[c], ss, sr, (dpi, sib))

    def far_part(us, t, h):
        zo = (z - t + nz) % nz
        return copy(psend.at[us, t, h], rbuf.at[us, t, c], ps.at[us, t, h], pr.at[us, t, c], (dpi, 2 * zo + h))

    def near_part(us):
        return copy(psend.at[us, 0, other], rbuf.at[us, 0, c], ps.at[us, 0, other], pr.at[us, 0, c], (dpi, sib))

    def near_dq(us):
        return copy(dqb.at[us, other], qg.at[2 * c + us], dqs.at[us], dqr.at[us], (dpi, sib))

    early = (z // 2) % 2

    @pl.loop(0, 2)
    def _(step):
        us = (step + early) % 2
        near_rows(us, 0).start()
        near_kv(us).start()
        near_rows(us, 1).start()

        @pl.loop(1, GROUP_CHIPS)
        def _(t):
            @pl.when(t <= slot(us, (z + t) % nz))
            def _():
                far_kv(us, t, 0).start()
                far_kv(us, t, 1).start()

    near_state().start()
    stb[c] = st[...]

    @pl.loop(0, 2)
    def _(us):
        qb[us, c] = q[2 * c + us]
        db[us, c] = d[2 * c + us]
        kvb[us, 0, c] = kv[2 * c + us]

    @pl.loop(0, 2)
    def _(step):
        us = (step + early) % 2
        nb = slot(us, z) + 1
        copy(kv.at[0], kvb.at[us, 0, other], kvs.at[us, 0, other], kvr.at[us, 0, other], (dpi, sib)).wait_recv()
        near_rows(us, 0).wait_recv()
        near_rows(us, 1).wait_recv()

        @pl.loop(1, nb)
        def _(t):
            for h in range(2):
                copy(kv.at[0], kvb.at[us, t, h], kvs.at[us, t, h], kvr.at[us, t, h], (dpi, sib)).wait_recv()

        @pl.loop(0, nb)
        def _(t):
            kT[t] = kvb[us, t, :, 0].reshape(2 * TOK, WIDTH).astype(F32).T.astype(BF16)
            acc[t] = jnp.zeros((2, 2 * TOK, WIDTH), F32)

        for count in range(1, GROUP_CHIPS + 1):
            @pl.when(nb == count)
            def _(count=count):
                @pl.loop(0, PER_GROUP // 2)
                def _(pair):
                    attend(count, us, pair, c, qb, db, kvb, kT, cosT, sinT, acc, dqb)

        @pl.loop(0, nb)
        def _(t):
            for h in range(2):
                psend[us, t, h] = acc[t, :, h * TOK : (h + 1) * TOK].astype(BF16)

        @pl.loop(1, nb)
        def _(t):
            far_part(us, t, 0).start()
            far_part(us, t, 1).start()

        near_part(us).start()
        near_dq(us).start()
        rbuf[us, 0, c] = psend[us, 0, c]
        qg[2 * c + us] = dqb[us, c]

        @pl.when(step == 0)
        def _():
            copy(st, stb.at[other], ss, sr, (dpi, sib)).wait_recv()

        part = dot(stb[0], dqb[us, 0], NN) + dot(stb[1], dqb[us, 1], NN)
        for j in range(nz // 2):
            qap[us * (nz // 2) + j] = part[:8, j * wide : (j + 1) * wide]

    def qz(k):
        return copy(qap.at[k], qzr.at[z], qzs_s.at[k], qzr_s.at[z], (dpi, 2 * k + c))

    @pl.loop(1, nz)
    def _(o):
        qz((z + o) % nz).start()

    qzr[z] = qap[z]

    @pl.loop(0, 2)
    def _(step):
        us = (step + early) % 2
        copy(kv.at[0], rbuf.at[us, 0, other], ps.at[us, 0, other], pr.at[us, 0, other], (dpi, sib)).wait_recv()
        for cc in range(2):
            own[us, cc] = rbuf[us, 0, cc].astype(F32)

        @pl.loop(1, GROUP_CHIPS)
        def _(t):
            @pl.when(t <= slot(us, (z + t) % nz))
            def _():
                for cc in range(2):
                    copy(kv.at[0], rbuf.at[us, t, cc], ps.at[us, t, cc], pr.at[us, t, cc], (dpi, sib)).wait_recv()
                    own[us, cc] += rbuf[us, t, cc].astype(F32)

    for cc in range(2):
        for us in range(2):
            place = 2 * cc + us
            dk = own[us, cc, 0] * SCORE_SCALE
            kg[place] = (dk * cosF[...] + pltpu.roll(dk, WIDTH // 2, 1) * sinF[...]).astype(BF16)
            dv = own[us, cc, 1].astype(BF16)
            vg[place] = dv
            vap[:, place * WIDTH : (place + 1) * WIDTH] = dot(st[...], dv, NN)[8:]

    def vz(o):
        return copy(vap, vzr.at[me], vzs_s.at[o], vzr_s.at[me], (dpi, (me + o) % n))

    @pl.loop(1, n)
    def _(o):
        vz(o).start()

    vzr[me] = vap[...]

    @pl.loop(1, nz)
    def _(o):
        k = (z + o) % nz
        copy(qap.at[k], qzr.at[k], qzs_s.at[k], qzr_s.at[k], (dpi, sib)).wait_recv()

    qds[...] = lax.fori_loop(0, nz, lambda k, x: x + qzr[k], jnp.zeros((8, wide), F32))

    def qd(o):
        return copy(qds, qdr.at[dpi], qds_s.at[o], qdr_s.at[dpi], ((dpi + o) % ndp, me))

    @pl.loop(1, ndp)
    def _(o):
        qd(o).start()

    qdr[dpi] = qds[...]

    @pl.loop(1, n)
    def _(o):
        k = (me + o) % n
        copy(vap, vzr.at[k], vzs_s.at[o], vzr_s.at[k], (dpi, sib)).wait_recv()

    vds[...] = lax.fori_loop(0, n, lambda k, x: x + vzr[k], jnp.zeros((8, KV_HEADS * WIDTH), F32))

    def vd(o):
        return copy(vds, vdr.at[dpi], vds_s.at[o], vdr_s.at[dpi], ((dpi + o) % ndp, me))

    @pl.loop(1, ndp)
    def _(o):
        vd(o).start()

    vdr[dpi] = vds[...]

    @pl.loop(1, ndp)
    def _(o):
        k = (dpi + o) % ndp
        copy(qds, qdr.at[k], qds_s.at[o], qdr_s.at[k], (dpi, sib)).wait_recv()

    qas[...] = lax.fori_loop(0, ndp, lambda k, x: x + qdr[k], jnp.zeros((8, wide), F32)) * ADAPTER_SCALE

    def qag(o):
        return copy(qas, qa.at[me], qas_s.at[o], qar_s.at[me], (dpi, (me + o) % n))

    @pl.loop(1, n)
    def _(o):
        qag(o).start()

    qa[me] = qas[...]

    @pl.loop(1, ndp)
    def _(o):
        k = (dpi + o) % ndp
        copy(vds, vdr.at[k], vds_s.at[o], vdr_s.at[k], (dpi, sib)).wait_recv()

    va[...] = (
        lax.fori_loop(0, ndp, lambda k, x: x + vdr[k], jnp.zeros((8, KV_HEADS * WIDTH), F32)) * ADAPTER_SCALE
    )

    @pl.loop(0, 2)
    def _(us):
        copy(dqb.at[us, other], qg.at[2 * other + us], dqs.at[us], dqr.at[us], (dpi, sib)).wait_recv()
        near_dq(us).wait_send()
        near_kv(us).wait_send()
        near_rows(us, 0).wait_send()
        near_rows(us, 1).wait_send()
        near_part(us).wait_send()

        @pl.loop(1, GROUP_CHIPS)
        def _(t):
            @pl.when(t <= slot(us, (z + t) % nz))
            def _():
                far_kv(us, t, 0).wait_send()
                far_kv(us, t, 1).wait_send()

            @pl.when(t <= slot(us, z))
            def _():
                far_part(us, t, 0).wait_send()
                far_part(us, t, 1).wait_send()

    near_state().wait_send()

    @pl.loop(1, nz)
    def _(o):
        qz((z + o) % nz).wait_send()

    @pl.loop(1, ndp)
    def _(o):
        qd(o).wait_send()
        vd(o).wait_send()

    @pl.loop(1, n)
    def _(o):
        vz(o).wait_send()
        qag(o).wait_send()
        k = (me + o) % n
        copy(qas, qa.at[k], qas_s.at[o], qar_s.at[k], (dpi, sib)).wait_recv()


def main_call(n, ndp, *operands):
    nz = n // 2
    wide = 2 * SPAN // nz
    vmem = pl.BlockSpec(memory_space=pltpu.VMEM)
    dma = pltpu.SemaphoreType.DMA
    hw = KV_HEADS * WIDTH
    return pl.pallas_call(
        functools.partial(main_kernel, n, ndp),
        in_specs=[vmem] * len(operands),
        out_specs=[vmem] * 5,
        out_shape=[
            jax.ShapeDtypeStruct((KV_HEADS, TOK, SPAN), BF16),
            jax.ShapeDtypeStruct((KV_HEADS, TOK, WIDTH), BF16),
            jax.ShapeDtypeStruct((KV_HEADS, TOK, WIDTH), BF16),
            jax.ShapeDtypeStruct((n, 8, wide), F32),
            jax.ShapeDtypeStruct((8, hw), F32),
        ],
        scratch_shapes=[
            pltpu.VMEM((2, 2, TOK, SPAN), BF16),
            pltpu.VMEM((2, 2, TOK, SPAN), BF16),
            pltpu.VMEM((2, GROUP_CHIPS, 2, 2, TOK, WIDTH), BF16),
            pltpu.VMEM((2, 16, TOK), BF16),
            pltpu.VMEM((GROUP_CHIPS, WIDTH, 2 * TOK), BF16),
            pltpu.VMEM((GROUP_CHIPS, 2, 2 * TOK, WIDTH), F32),
            pltpu.VMEM((2, GROUP_CHIPS, 2, 2, TOK, WIDTH), BF16),
            pltpu.VMEM((2, GROUP_CHIPS, 2, 2, TOK, WIDTH), BF16),
            pltpu.VMEM((2, 2, TOK, SPAN), BF16),
            pltpu.VMEM((2, 2, 2, TOK, WIDTH), F32),
            pltpu.VMEM((nz, 8, wide), F32),
            pltpu.VMEM((nz, 8, wide), F32),
            pltpu.VMEM((8, wide), F32),
            pltpu.VMEM((ndp, 8, wide), F32),
            pltpu.VMEM((8, wide), F32),
            pltpu.VMEM((8, hw), F32),
            pltpu.VMEM((n, 8, hw), F32),
            pltpu.VMEM((8, hw), F32),
            pltpu.VMEM((ndp, 8, hw), F32),
            dma((2, GROUP_CHIPS, 2)), dma((2, GROUP_CHIPS, 2)),
            dma((2, 2)), dma((2, 2)),
            dma, dma,
            dma((2, GROUP_CHIPS, 2)), dma((2, GROUP_CHIPS, 2)),
            dma((2,)), dma((2,)),
            dma((nz,)), dma((nz,)),
            dma((ndp,)), dma((ndp,)),
            dma((n,)), dma((n,)),
            dma((n,)), dma((n,)),
            dma((ndp,)), dma((ndp,)),
        ],
        compiler_params=pltpu.CompilerParams(
            collective_id=0, has_side_effects=True, vmem_limit_bytes=56 * 1024 * 1024
        ),
        name="attention_backward",
    )(*operands)


def local(n, ndp, query, keys, values, out_grad, query_state, value_state, flags):
    nz = n // 2
    wide = 2 * SPAN // nz
    me = lax.axis_index("ctx")
    z = me // 2
    heads = jnp.arange(KV_HEADS, dtype=jnp.int32)
    before = heads[None, :] < heads[:, None]
    same = flags[None, :] == flags[:, None]
    place = 2 * jnp.sum(before & same, axis=1, dtype=jnp.int32) + flags
    order = jnp.sum(jnp.where(place[None, :] == heads[:, None], heads[None, :], 0), axis=1, dtype=jnp.int32)

    half = WIDTH // 2
    inv_freq = 10000.0 ** (-(jnp.arange(half, dtype=F32) * 2.0) / WIDTH)
    chip_pos = (z * 2 * TOK + jnp.arange(2 * TOK, dtype=jnp.int32)).astype(F32)
    angleT = inv_freq[:, None] * chip_pos[None, :]
    cosT = jnp.cos(angleT)
    sinT = jnp.sin(angleT)
    cos_own = lax.dynamic_slice(cosT, (0, (me % 2) * TOK), (half, TOK)).T
    sin_own = lax.dynamic_slice(sinT, (0, (me % 2) * TOK), (half, TOK)).T
    cosF = jnp.concatenate([cos_own, cos_own], axis=1)
    sinF = jnp.concatenate([sin_own, -sin_own], axis=1)
    state = jnp.concatenate([query_state[0], value_state[0]], axis=1).T

    q4, d4, kv4 = arrange(order, query[0], out_grad[0], keys[0], values[0])
    qg, kg, vg, qa, va = main_call(n, ndp, q4, d4, kv4, state, cosT, sinT, cosF, sinF)
    qa = qa.reshape(nz, 2, 8, wide).transpose(2, 1, 0, 3).reshape(8, KV_HEADS * SPAN)
    qg, kg, vg, qa, va = restore(place, qg, kg, vg, qa, va)
    return qg[None], kg[None], vg[None], qa, va


def solution(mesh):
    split = P("dp", "ctx", None)
    return jax.shard_map(
        functools.partial(local, mesh.shape["ctx"], mesh.shape["dp"]),
        mesh=mesh,
        in_specs=(split,) * 6 + (P(),),
        out_specs=(split, split, split, P(), P()),
        check_vma=False,
    )
```

profile of v0, /device:TPU:0, one launch (start us, length us, event | category | flops | bytes accessed | tf_op | source)
XLA Modules:
  0.0 68.3 jit_solution(16049357923873062)
XLA Ops:
  0.7 0.0 copy-start.3
  0.7 0.6 copy-done.3
  1.3 0.2 convert_reduce_fusion
  1.5 0.0 copy-start.2
  1.5 0.0 copy-start.1
  1.5 0.6 select_reduce_fusion.order
  2.1 0.0 copy-done.2
  2.1 0.0 copy-start
  2.2 0.0 copy-done.1
  2.2 0.6 copy-done
  2.8 0.6 maximum_bitcast_fusion.st
  3.4 0.5 multiply_sine_fusion
  4.0 0.7 %copy.20.sinT = f32[64,256]{1,0:T(8,128)} copy(f32[64,256]{0,1:T(8,128)S(1)} %get-tuple-element.33) | data formatting | bytes 131072 | tf_op jit(solution)/shard_map/sin | solution.py:501
  4.7 0.7 %copy.19.cosT = f32[64,256]{1,0:T(8,128)} copy(f32[64,256]{0,1:T(8,128)S(1)} %get-tuple-element.34) | data formatting | bytes 131072 | tf_op jit(solution)/shard_map/cos | solution.py:500
  5.4 0.8 %pad_maximum_fusion = (f32[128,128]{1,0:T(8,128)}, f32[128,128]{1,0:T(8,128)}) fusion(f32[128,64]{1,0:T(8,128)S(1)} %dynamic-slice_bitcast_fusion.1, f32[128,64]{1,0:T(8,128)S(1)} %get-tuple-element.31, f32[128,64]{1,0:T(8,128)S(1)} %get-tuple-element.32), kind=kLoop, calls=%fused_computation.2 | loop fusion | flops 32768 | bytes 229376 | tf_op jit(solution)/shard_map/concatenate | solution.py:504
  6.2 4.5 %arrange_heads.1 = (bf16[4,128,1024]{2,1,0:T(8,128)(2,1)}, bf16[4,128,1024]{2,1,0:T(8,128)(2,1)}, bf16[4,2,128,128]{3,2,1,0:T(8,128)(2,1)}) custom-call(s32[4]{0:T(128)} %select_reduce_fusion.order, bf16[128,4096]{1,0:T(8,128)(2,1)} %bitcast.20, bf16[128,4096]{1,0:T(8,128)(2,1)} %bitcast.21, bf16[128,512]{1,0:T(8,128)(2,1)} %bitcast.23, ...), custom_call_target="tpu_custom_call" | custom-call | tf_op jit(solution)/shard_map/arrange_heads/pallas_call | solution.py:48
  10.6 51.9 %attention_backward.1 = (bf16[4,128,1024]{2,1,0:T(8,128)(2,1)}, bf16[4,128,128]{2,1,0:T(8,128)(2,1)}, bf16[4,128,128]{2,1,0:T(8,128)(2,1)}, f32[8,8,512]{2,1,0:T(8,128)}, f32[8,512]{1,0:T(8,128)}) custom-call(bf16[4,128,1024]{2,1,0:T(8,128)(2,1)} %get-tuple-element.18.q, bf16[4,128,1024]{2,1,0:T(8,128)(2,1)} %get-tuple-element.19.d, ...), custom_call_target="tpu_custom_call" | custom-call | tf_op jit(solution)/shard_map/attention_backward/pallas_call | solution.py:436
  62.6 1.6 %copy.21 = f32[4,2,8,512]{3,2,0,1:T(8,128)} copy(f32[4,2,8,512]{3,2,1,0:T(8,128)} %bitcast.25) | data formatting | bytes 262144 | tf_op jit(solution)/shard_map/reshape | solution.py:510
  64.1 4.2 %restore_heads.1 = (bf16[128,4096]{1,0:T(8,128)(2,1)}, bf16[128,512]{1,0:T(8,128)(2,1)}, bf16[128,512]{1,0:T(8,128)(2,1)}, f32[8,4096]{1,0:T(8,128)}, f32[8,512]{1,0:T(8,128)}) custom-call(s32[4]{0:T(128)} %copy-done.2, bf16[4,128,1024]{2,1,0:T(8,128)(2,1)} %get-tuple-element.21.q, bf16[4,128,128]{2,1,0:T(8,128)(2,1)} %get-tuple-element.22.k, ...), custom_call_target="tpu_custom_call" | custom-call | tf_op jit(solution)/shard_map/restore_heads/pallas_call | solution.py:89
  (5 shorter events, 0.0 us)
Async XLA Ops:
  0.7 0.7 copy-start.3
  1.5 0.6 copy-start.2
  1.5 0.7 %copy-start.1 = (bf16[1,128,8]{1,2,0:T(8,128)(2,1)S(1)}, bf16[1,128,8]{1,2,0:T(8,128)(2,1)}, u32[]{:S(2)}) copy-start(bf16[1,128,8]{1,2,0:T(8,128)(2,1)} %param.11) | copy-start | bytes 6148
  2.1 0.7 copy-start
where the time goes:
time: 68.7 us; the launch traced here: 68.3 us
  Pallas kernels  60.6 us (88%)
  local copies, waits for them, and re-layouts  4.32 us (6%)
  other arithmetic  2.71 us (4%)
  between operations  0.71 us (1%)
    pallas_call x1, Pallas kernels, main_call(): pl.pallas_call(functools.partial(main_kernel, n, ndp), in_specs=[vmem] *...  51.9 us
    pallas_call x1, Pallas kernels, arrange(): pl.pallas_call(arrange_kernel, grid_spec=spec, out_shape=[jax.ShapeDtypeS...  4.48 us
    pallas_call x1, Pallas kernels, restore(): pl.pallas_call(restore_kernel, grid_spec=spec, out_shape=[jax.ShapeDtypeS...  4.2 us
    reshape x1, local copies, waits for them, and re-layouts, local(): qa.reshape(nz, 2, 8, wide).transpose(2, 1, 0, 3).reshape(8, KV_HEADS * SPAN)  1.56 us

commit v1 on v0

v1 whole, which is shorter than its diff:
```python
import functools
import math

import jax
import jax.numpy as jnp
from jax import lax
from jax.experimental import pallas as pl
from jax.experimental.pallas import tpu as pltpu
from jax.sharding import PartitionSpec as P
import numpy as np

KV_HEADS = 4
PER_GROUP = 8
WIDTH = 128
TOK = 128
GROUP_CHIPS = 4
SPAN = PER_GROUP * WIDTH
ADAPTER_SCALE = 2.0
SCORE_SCALE = 1.0 / math.sqrt(WIDTH)
EXP2_SCALE = SCORE_SCALE * math.log2(math.e)
MESH = pl.DeviceIdType.MESH
F32 = jnp.float32
BF16 = jnp.bfloat16


def dot(a, b, dims):
    return lax.dot_general(a, b, (dims, ((), ())), preferred_element_type=F32)


NT = ((1,), (1,))
NN = ((1,), (0,))


def attend(nb, us, pair, qb, db, kvb, kT, table, acc, dqb):
    span = nb * 2 * TOK
    cols = [pl.ds(pl.multiple_of(pair * 2 * WIDTH + g * WIDTH, WIDTH), WIDTH) for g in range(2)]
    rows_q = jnp.concatenate([qb[us, h, :, cols[g]] for g in range(2) for h in range(2)], axis=0)
    rows_d = jnp.concatenate([db[us, h, :, cols[g]] for g in range(2) for h in range(2)], axis=0)
    n_rows = 4 * TOK
    key = kvb[us, 0:nb, :, 0].reshape(span, WIDTH)
    val = kvb[us, 0:nb, :, 1].reshape(span, WIDTH)
    score = dot(key, rows_q, NT)
    kpos = lax.broadcasted_iota(jnp.int32, (2 * TOK, n_rows), 0)
    rpos = lax.broadcasted_iota(jnp.int32, (2 * TOK, n_rows), 1) & (2 * TOK - 1)
    diagonal = jnp.where(kpos <= rpos, score[: 2 * TOK], -jnp.inf)
    score = diagonal if nb == 1 else jnp.concatenate([diagonal, score[2 * TOK :]], axis=0)
    dprob = dot(val, rows_d, NT)
    top = jnp.max(score, axis=0, keepdims=True)
    weight = jnp.exp2((score - top) * EXP2_SCALE)
    total = jnp.sum(weight, axis=0, keepdims=True)
    mixed = jnp.sum(weight * dprob, axis=0, keepdims=True)
    inverse = 1.0 / total
    delta = mixed * inverse
    prob = weight * inverse
    ds = (prob * (dprob - delta)).astype(BF16)
    acc[1, :span] += dot(prob.astype(BF16), rows_d, NN)
    acc[0, :span] += dot(ds, rows_q, NN)
    dqT = dot(kT[:, :span], ds, NN)
    cos = jnp.concatenate([table[0], table[0]], axis=1)
    sin = jnp.concatenate([table[1], table[1]], axis=1)
    front = dqT[: WIDTH // 2] * SCORE_SCALE
    back = dqT[WIDTH // 2 :] * SCORE_SCALE
    turned = jnp.concatenate([front * cos + back * sin, back * cos - front * sin], axis=0)
    dq = turned.T.astype(BF16)
    for g in range(2):
        for h in range(2):
            at = (g * 2 + h) * TOK
            dqb[us, h, :, cols[g]] = dq[at : at + TOK]


def main_kernel(
    n, ndp,
    flags, q_hbm, d_hbm, k_in, v_in, sq, sv, tables,
    qg, kg, vg, qa, va,
    q, d, table, qsend, dsend, kv,
    qb, db, kvb, st, stb, kT, acc, psend, rbuf, dqb, qgs, own,
    vpart, msg, zr, zsum, dr, res, gat,
    loads, kvs, kvr, qs, qr, ss, sr, ps, pr, dqs, dqr,
    zs_s, zr_s, ds_s, dr_s, as_s, ar_s,
):
    nz = n // 2
    wide = 2 * SPAN // nz
    me = lax.axis_index("ctx")
    dpi = lax.axis_index("dp")
    z = me // 2
    c = me % 2
    other = 1 - c
    sib = z * 2 + other

    def slot(us, zz):
        return (zz + 2 * us) % GROUP_CHIPS

    def copy(src, dst, send, recv, target):
        return pltpu.make_async_remote_copy(
            src_ref=src, dst_ref=dst, send_sem=send, recv_sem=recv,
            device_id=target, device_id_type=MESH,
        )

    load_q = pltpu.make_async_copy(q_hbm, q, loads.at[0])
    load_d = pltpu.make_async_copy(d_hbm, d, loads.at[1])
    load_t = pltpu.make_async_copy(tables.at[z], table, loads.at[2])
    load_q.start()
    load_d.start()
    load_t.start()

    barrier = pltpu.get_barrier_semaphore()

    @pl.loop(1, n)
    def _(o):
        pl.semaphore_signal(barrier, inc=1, device_id=(dpi, (me + o) % n), device_id_type=MESH)

    @pl.loop(1, ndp)
    def _(o):
        pl.semaphore_signal(barrier, inc=1, device_id=((dpi + o) % ndp, me), device_id_type=MESH)

    flag = [flags[h] for h in range(KV_HEADS)]

    def same(a, b):
        return 1 - (a - b) * (a - b)

    rank = [sum((same(flag[j], flag[h]) for j in range(h)), jnp.int32(0)) for h in range(KV_HEADS)]

    def share(h, cc, us):
        return (same(rank[h], cc) * same(flag[h], us)).astype(F32)

    def pick(parts, weights):
        total = None
        for part, weight in zip(parts, weights):
            term = part * jnp.full(part.shape, weight, F32).astype(part.dtype)
            total = term if total is None else total + term
        return total

    def gather(ref, width, cc, us):
        heads = range(KV_HEADS)
        return pick([ref[:, h * width : (h + 1) * width] for h in heads], [share(h, cc, us) for h in heads])

    st[...] = jnp.concatenate([sq[...].astype(F32), sv[...].astype(F32)], axis=0).astype(BF16)
    stb[0, c] = st[...]
    for s in range(KV_HEADS):
        kv[s, 0] = gather(k_in, WIDTH, s // 2, s % 2)
        kv[s, 1] = gather(v_in, WIDTH, s // 2, s % 2)
    early = (z // 2) % 2
    load_q.wait()
    load_d.wait()
    for us in range(2):
        qsend[us] = gather(q, SPAN, other, us)
        dsend[us] = gather(d, SPAN, other, us)
        qb[us, c] = gather(q, SPAN, c, us)
        db[us, c] = gather(d, SPAN, c, us)
        kvb[us, 0, c] = kv[2 * c + us]
    load_t.wait()

    pl.semaphore_wait(barrier, n - 1 + ndp - 1)

    def near_kv(us):
        return copy(kv.at[2 * other + us], kvb.at[us, 0, c], kvs.at[us, 0, other], kvr.at[us, 0, c], (dpi, sib))

    def far_kv(us, t, cc):
        zt = (z + t) % nz
        return copy(kv.at[2 * cc + us], kvb.at[us, t, c], kvs.at[us, t, cc], kvr.at[us, t, c], (dpi, 2 * zt + cc))

    def near_rows(us, i):
        src, dst = ((qsend, qb), (dsend, db))[i]
        return copy(src.at[us], dst.at[us, c], qs.at[us, i], qr.at[us, i], (dpi, sib))

    def near_state():
        return copy(st, stb.at[0, c], ss.at[0, other], sr.at[0, c], (dpi, sib))

    def far_state(t, cc):
        zt = (z + t) % nz
        return copy(st, stb.at[t, c], ss.at[t, cc], sr.at[t, c], (dpi, 2 * zt + cc))

    def far_part(us, t, h):
        zo = (z - t + nz) % nz
        return copy(psend.at[us, t, h], rbuf.at[us, t, c], ps.at[us, t, h], pr.at[us, t, c], (dpi, 2 * zo + h))

    def near_part(us):
        return copy(psend.at[us, 0, other], rbuf.at[us, 0, c], ps.at[us, 0, other], pr.at[us, 0, c], (dpi, sib))

    def near_dq(us):
        return copy(dqb.at[us, other], qgs.at[2 * c + us], dqs.at[us], dqr.at[us], (dpi, sib))

    @pl.loop(0, 2)
    def _(step):
        us = (step + early) % 2
        near_kv(us).start()
        near_rows(us, 0).start()
        near_rows(us, 1).start()

        @pl.loop(1, GROUP_CHIPS)
        def _(t):
            @pl.when(t <= slot(us, (z + t) % nz))
            def _():
                far_kv(us, t, 0).start()
                far_kv(us, t, 1).start()

    near_state().start()

    @pl.loop(1, GROUP_CHIPS)
    def _(t):
        far_state(t, 0).start()
        far_state(t, 1).start()

    @pl.loop(0, 2)
    def _(step):
        us = (step + early) % 2
        nb = slot(us, z) + 1
        copy(kv.at[0], kvb.at[us, 0, other], kvs.at[us, 0, other], kvr.at[us, 0, other], (dpi, sib)).wait_recv()
        near_rows(us, 0).wait_recv()
        near_rows(us, 1).wait_recv()

        @pl.loop(1, nb)
        def _(t):
            for h in range(2):
                copy(kv.at[0], kvb.at[us, t, h], kvs.at[us, t, h], kvr.at[us, t, h], (dpi, sib)).wait_recv()

        @pl.loop(0, nb)
        def _(t):
            at = pl.ds(pl.multiple_of(t * 2 * TOK, 2 * TOK), 2 * TOK)
            kT[:, at] = kvb[us, t, :, 0].reshape(2 * TOK, WIDTH).astype(F32).T.astype(BF16)
            acc[0, at] = jnp.zeros((2 * TOK, WIDTH), F32)
            acc[1, at] = jnp.zeros((2 * TOK, WIDTH), F32)

        for count in range(1, GROUP_CHIPS + 1):
            @pl.when(nb == count)
            def _(count=count):
                @pl.loop(0, PER_GROUP // 2)
                def _(pair):
                    attend(count, us, pair, qb, db, kvb, kT, table, acc, dqb)

        near_dq(us).start()

        @pl.loop(0, nb)
        def _(t):
            for h in range(2):
                at = pl.ds(pl.multiple_of(t * 2 * TOK + h * TOK, TOK), TOK)
                psend[us, t, h, 0] = acc[0, at].astype(BF16)
                psend[us, t, h, 1] = acc[1, at].astype(BF16)

            @pl.when(t > 0)
            def _():
                far_part(us, t, 0).start()
                far_part(us, t, 1).start()

        near_part(us).start()

        @pl.when(step == 0)
        def _():
            copy(st, stb.at[0, other], ss.at[0, other], sr.at[0, other], (dpi, sib)).wait_recv()

            @pl.loop(1, GROUP_CHIPS)
            def _(t):
                for h in range(2):
                    copy(st, stb.at[t, h], ss.at[t, h], sr.at[t, h], (dpi, sib)).wait_recv()

        part = dot(stb[0, 0], dqb[us, 0], NN) + dot(stb[0, 1], dqb[us, 1], NN)
        for j in range(nz // 2):
            msg[us * (nz // 2) + j, :, :wide] = part[:8, j * wide : (j + 1) * wide]

        def value_term(t, x):
            return x + dot(stb[t, 0], psend[us, t, 0, 1], NN) + dot(stb[t, 1], psend[us, t, 1, 1], NN)

        vpart[us] = lax.fori_loop(0, nb, value_term, jnp.zeros((16, WIDTH), F32))
        rbuf[us, 0, c] = psend[us, 0, c]
        qgs[2 * c + us] = dqb[us, c]

    for k in range(nz):
        for us in range(2):
            msg[k, :, wide + us * WIDTH : wide + (us + 1) * WIDTH] = vpart[us, 8:]

    def to_chip(k):
        return copy(msg.at[k], zr.at[z], zs_s.at[k], zr_s.at[z], (dpi, 2 * k + c))

    @pl.loop(1, nz)
    def _(o):
        to_chip((z + o) % nz).start()

    zr[z] = msg[z]

    @pl.loop(1, nz)
    def _(o):
        k = (z + o) % nz
        copy(msg.at[k], zr.at[k], zs_s.at[k], zr_s.at[k], (dpi, sib)).wait_recv()

    zsum[...] = lax.fori_loop(0, nz, lambda k, x: x + zr[k], jnp.zeros((8, wide + 2 * WIDTH), F32))

    def to_dp(o):
        return copy(zsum, dr.at[dpi], ds_s.at[o], dr_s.at[dpi], ((dpi + o) % ndp, me))

    @pl.loop(1, ndp)
    def _(o):
        to_dp(o).start()

    dr[dpi] = zsum[...]

    def owner_sum(us):
        copy(kv.at[0], rbuf.at[us, 0, other], ps.at[us, 0, other], pr.at[us, 0, other], (dpi, sib)).wait_recv()
        for cc in range(2):
            own[us, cc] = rbuf[us, 0, cc].astype(F32)

        @pl.loop(1, GROUP_CHIPS)
        def _(t):
            @pl.when(t <= slot(us, (z + t) % nz))
            def _():
                for cc in range(2):
                    copy(kv.at[0], rbuf.at[us, t, cc], ps.at[us, t, cc], pr.at[us, t, cc], (dpi, sib)).wait_recv()
                    own[us, cc] += rbuf[us, t, cc].astype(F32)

    @pl.loop(1, ndp)
    def _(o):
        k = (dpi + o) % ndp
        copy(zsum, dr.at[k], ds_s.at[o], dr_s.at[k], (dpi, sib)).wait_recv()

    res[...] = (
        lax.fori_loop(0, ndp, lambda k, x: x + dr[k], jnp.zeros((8, wide + 2 * WIDTH), F32)) * ADAPTER_SCALE
    )

    def to_ctx(o):
        return copy(res, gat.at[me], as_s.at[o], ar_s.at[me], (dpi, (me + o) % n))

    @pl.loop(1, n)
    def _(o):
        to_ctx(o).start()

    gat[me] = res[...]

    def spread(h):
        return [share(h, s // 2, s % 2) for s in range(KV_HEADS)]

    @pl.loop(0, 2)
    def _(us):
        copy(dqb.at[us, other], qgs.at[2 * other + us], dqs.at[us], dqr.at[us], (dpi, sib)).wait_recv()

    for h in range(KV_HEADS):
        qg[:, h * SPAN : (h + 1) * SPAN] = pick([qgs[s] for s in range(KV_HEADS)], spread(h))

    @pl.loop(0, 2)
    def _(us):
        owner_sum(us)

    cos = jnp.where(c == 0, table[0, :, :TOK], table[0, :, TOK:]).T
    sin = jnp.where(c == 0, table[1, :, :TOK], table[1, :, TOK:]).T
    cos = jnp.concatenate([cos, cos], axis=1)
    sin = jnp.concatenate([sin, -sin], axis=1)
    for h in range(KV_HEADS):
        at = slice(h * WIDTH, (h + 1) * WIDTH)
        dk = pick([own[s % 2, s // 2, 0] for s in range(KV_HEADS)], spread(h)) * SCORE_SCALE
        kg[:, at] = (dk * cos + pltpu.roll(dk, WIDTH // 2, 1) * sin).astype(BF16)
        vg[:, at] = pick([own[s % 2, s // 2, 1] for s in range(KV_HEADS)], spread(h)).astype(BF16)

    @pl.loop(1, n)
    def _(o):
        k = (me + o) % n
        copy(res, gat.at[k], as_s.at[o], ar_s.at[k], (dpi, sib)).wait_recv()

    for h in range(KV_HEADS):
        for j in range(nz // 2):
            at = h * SPAN + j * wide
            held = [gat[2 * (s % 2 * (nz // 2) + j) + s // 2, :, :wide] for s in range(KV_HEADS)]
            qa[:, at : at + wide] = pick(held, spread(h))
        held = [gat[s // 2, :, wide + s % 2 * WIDTH : wide + (s % 2 + 1) * WIDTH] for s in range(KV_HEADS)]
        va[:, h * WIDTH : (h + 1) * WIDTH] = pick(held, spread(h))

    @pl.loop(0, 2)
    def _(us):
        near_dq(us).wait_send()
        near_kv(us).wait_send()
        near_rows(us, 0).wait_send()
        near_rows(us, 1).wait_send()
        near_part(us).wait_send()

        @pl.loop(1, GROUP_CHIPS)
        def _(t):
            @pl.when(t <= slot(us, (z + t) % nz))
            def _():
                far_kv(us, t, 0).wait_send()
                far_kv(us, t, 1).wait_send()

            @pl.when(t <= slot(us, z))
            def _():
                far_part(us, t, 0).wait_send()
                far_part(us, t, 1).wait_send()

    near_state().wait_send()

    @pl.loop(1, GROUP_CHIPS)
    def _(t):
        far_state(t, 0).wait_send()
        far_state(t, 1).wait_send()

    @pl.loop(1, nz)
    def _(o):
        to_chip((z + o) % nz).wait_send()

    @pl.loop(1, ndp)
    def _(o):
        to_dp(o).wait_send()

    @pl.loop(1, n)
    def _(o):
        to_ctx(o).wait_send()


def main_call(n, ndp, *operands):
    nz = n // 2
    line = 2 * SPAN // nz + 2 * WIDTH
    vmem = pl.BlockSpec(memory_space=pltpu.VMEM)
    smem = pl.BlockSpec(memory_space=pltpu.SMEM)
    away = pl.BlockSpec(memory_space=pl.ANY)
    dma = pltpu.SemaphoreType.DMA
    hw = KV_HEADS * WIDTH
    return pl.pallas_call(
        functools.partial(main_kernel, n, ndp),
        in_specs=[smem, away, away, vmem, vmem, vmem, vmem, away],
        out_specs=[vmem] * 5,
        out_shape=[
            jax.ShapeDtypeStruct((TOK, KV_HEADS * SPAN), BF16),
            jax.ShapeDtypeStruct((TOK, hw), BF16),
            jax.ShapeDtypeStruct((TOK, hw), BF16),
            jax.ShapeDtypeStruct((8, KV_HEADS * SPAN), F32),
            jax.ShapeDtypeStruct((8, hw), F32),
        ],
        scratch_shapes=[
            pltpu.VMEM((TOK, KV_HEADS * SPAN), BF16),
            pltpu.VMEM((TOK, KV_HEADS * SPAN), BF16),
            pltpu.VMEM((2, WIDTH // 2, 2 * TOK), F32),
            pltpu.VMEM((2, TOK, SPAN), BF16),
            pltpu.VMEM((2, TOK, SPAN), BF16),
            pltpu.VMEM((KV_HEADS, 2, TOK, WIDTH), BF16),
            pltpu.VMEM((2, 2, TOK, SPAN), BF16),
            pltpu.VMEM((2, 2, TOK, SPAN), BF16),
            pltpu.VMEM((2, GROUP_CHIPS, 2, 2, TOK, WIDTH), BF16),
            pltpu.VMEM((16, TOK), BF16),
            pltpu.VMEM((GROUP_CHIPS, 2, 16, TOK), BF16),
            pltpu.VMEM((WIDTH, GROUP_CHIPS * 2 * TOK), BF16),
            pltpu.VMEM((2, GROUP_CHIPS * 2 * TOK, WIDTH), F32),
            pltpu.VMEM((2, GROUP_CHIPS, 2, 2, TOK, WIDTH), BF16),
            pltpu.VMEM((2, GROUP_CHIPS, 2, 2, TOK, WIDTH), BF16),
            pltpu.VMEM((2, 2, TOK, SPAN), BF16),
            pltpu.VMEM((KV_HEADS, TOK, SPAN), BF16),
            pltpu.VMEM((2, 2, 2, TOK, WIDTH), F32),
            pltpu.VMEM((2, 16, WIDTH), F32),
            pltpu.VMEM((nz, 8, line), F32),
            pltpu.VMEM((nz, 8, line), F32),
            pltpu.VMEM((8, line), F32),
            pltpu.VMEM((ndp, 8, line), F32),
            pltpu.VMEM((8, line), F32),
            pltpu.VMEM((n, 8, line), F32),
            dma((3,)),
            dma((2, GROUP_CHIPS, 2)), dma((2, GROUP_CHIPS, 2)),
            dma((2, 2)), dma((2, 2)),
            dma((GROUP_CHIPS, 2)), dma((GROUP_CHIPS, 2)),
            dma((2, GROUP_CHIPS, 2)), dma((2, GROUP_CHIPS, 2)),
            dma((2,)), dma((2,)),
            dma((nz,)), dma((nz,)),
            dma((ndp,)), dma((ndp,)),
            dma((n,)), dma((n,)),
        ],
        compiler_params=pltpu.CompilerParams(
            collective_id=0, has_side_effects=True, vmem_limit_bytes=56 * 1024 * 1024
        ),
        name="attention_backward",
    )(*operands)


def position_tables(n):
    half = WIDTH // 2
    inv_freq = 10000.0 ** (-(np.arange(half) * 2.0) / WIDTH)
    angle = inv_freq[None, :, None] * np.arange(n * TOK).reshape(n // 2, 1, 2 * TOK)
    return np.stack([np.cos(angle), np.sin(angle)], axis=1).astype(np.float32)


def local(n, ndp, query, keys, values, out_grad, query_state, value_state, flags):
    tables = jnp.asarray(position_tables(n))
    qg, kg, vg, qa, va = main_call(
        n, ndp, flags, query[0], out_grad[0], keys[0], values[0], query_state[0].T, value_state[0].T, tables
    )
    return qg[None], kg[None], vg[None], qa, va


def solution(mesh):
    split = P("dp", "ctx", None)
    return jax.shard_map(
        functools.partial(local, mesh.shape["ctx"], mesh.shape["dp"]),
        mesh=mesh,
        in_specs=(split,) * 6 + (P(),),
        out_specs=(split, split, split, P(), P()),
        check_vma=False,
    )
```

time: 68.7 us -> 60.5 us (0.88)
  Pallas kernels: 60.6 us -> 54.1 us
  other arithmetic: 2.71 us -> 0 us
  local copies, waits for them, and re-layouts: 4.32 us -> 5.55 us
    pallas_call x3 -> x1, Pallas kernels: 60.6 us -> 54.1 us  [main_call(): pl.pallas_call(functools.partial(main_kernel, n, ndp), in_specs=[smem, aw...]
    unnamed x8 -> x13, local copies, waits for them, and re-layouts: 1.32 us -> 5.55 us
    reshape x1 -> x0, local copies, waits for them, and re-layouts: 1.56 us -> none  [local(): qa.reshape(nz, 2, 8, wide).transpose(2, 1, 0, 3).reshape(8, KV_HEADS * SPAN)]
    reduce_sum x2 -> x0, other arithmetic: 0.8 us -> none  [the longest x1 0.62 us: local(): jnp.sum(jnp.where(place[None, :] == heads[:, None], heads[None, :], 0), a...]
    concatenate x1 -> x0, other arithmetic: 0.75 us -> none  [local(): cosF = jnp.concatenate([cos_own, cos_own], axis=1)]
    sin x1 -> x0, local copies, waits for them, and re-layouts: 0.71 us -> none  [local(): sinT = jnp.sin(angleT)]
    cos x1 -> x0, local copies, waits for them, and re-layouts: 0.71 us -> none  [local(): cosT = jnp.cos(angleT)]
where the time goes in v1:
time: 60.5 us; the launch traced here: 60.3 us
  Pallas kernels  54.1 us (89%)
  local copies, waits for them, and re-layouts  5.55 us (9%)
  between operations  0.66 us (1%)
    pallas_call x1, Pallas kernels, main_call(): pl.pallas_call(functools.partial(main_kernel, n, ndp), in_specs=[smem, aw...  54.1 us
    unnamed x13, local copies, waits for them, and re-layouts  5.55 us

profile of v1, /device:TPU:0, one launch (start us, length us, event | category | flops | bytes accessed | tf_op | source)
XLA Modules:
  0.0 60.3 jit_solution(972033916251738831)
XLA Ops:
  0.6 54.1 %attention_backward.1 = (bf16[128,4096]{1,0:T(8,128)(2,1)}, bf16[128,512]{1,0:T(8,128)(2,1)}, bf16[128,512]{1,0:T(8,128)(2,1)}, f32[8,4096]{1,0:T(8,128)}, f32[8,512]{1,0:T(8,128)}) custom-call(s32[4]{0:T(128)} %flags.1, bf16[128,4096]{1,0:T(8,128)(2,1)} %bitcast.13, bf16[128,4096]{1,0:T(8,128)(2,1)} %bitcast.14, bf16[128,512]{1,0:T(8,128)(2,1)} %bitcast.16, ...), custom_call_target="tpu_custom_call" | custom-call | tf_op jit(solution)/shard_map/attention_backward/pallas_call | solution.py:412
  54.7 0.0 copy-start.2
  54.7 2.3 %copy.18 = bf16[1,128,4096]{2,1,0:T(8,128)(2,1)} copy(bf16[1,128,4096]{2,1,0:T(8,128)(2,1)} %bitcast.15) | data formatting | bytes 2097152
  57.0 0.0 copy-done.2
  57.0 0.0 copy-start.1
  57.0 0.7 %copy.19 = bf16[1,128,512]{2,1,0:T(8,128)(2,1)} copy(bf16[1,128,512]{2,1,0:T(8,128)(2,1)S(1)} %bitcast.19) | data formatting | bytes 262144
  57.7 0.3 copy-done.1
  58.0 0.0 copy-start
  58.0 0.7 %copy.20 = bf16[1,128,512]{2,1,0:T(8,128)(2,1)} copy(bf16[1,128,512]{2,1,0:T(8,128)(2,1)S(1)} %bitcast.18) | data formatting | bytes 262144
  58.6 0.3 copy-done
  58.9 0.0 copy-start.3
  58.9 0.7 %copy.21 = f32[8,4096]{1,0:T(8,128)} copy(f32[8,4096]{1,0:T(8,128)S(1)} %copy-done) | data formatting | bytes 262144
  59.6 0.1 copy-done.3
  59.7 0.6 %copy.22 = f32[8,512]{1,0:T(8,128)} copy(f32[8,512]{1,0:T(8,128)S(1)} %copy-done.3) | data formatting | bytes 32768
Async XLA Ops:
  54.7 2.3 %copy-start.2 = (bf16[128,512]{1,0:T(8,128)(2,1)S(1)}, bf16[128,512]{1,0:T(8,128)(2,1)}, u32[]{:S(2)}) copy-start(bf16[128,512]{1,0:T(8,128)(2,1)} %get-tuple-element.11) | copy-start | bytes 393220
  57.0 1.0 %copy-start.1 = (bf16[128,512]{1,0:T(8,128)(2,1)S(1)}, bf16[128,512]{1,0:T(8,128)(2,1)}, u32[]{:S(2)}) copy-start(bf16[128,512]{1,0:T(8,128)(2,1)} %get-tuple-element.12) | copy-start | bytes 393220
  58.0 1.0 %copy-start = (f32[8,4096]{1,0:T(8,128)S(1)}, f32[8,4096]{1,0:T(8,128)}, u32[]{:S(2)}) copy-start(f32[8,4096]{1,0:T(8,128)} %get-tuple-element.23) | copy-start | bytes 393220
  58.9 0.7 %copy-start.3 = (f32[8,512]{1,0:T(8,128)S(1)}, f32[8,512]{1,0:T(8,128)}, u32[]{:S(2)}) copy-start(f32[8,512]{1,0:T(8,128)} %get-tuple-element.24) | copy-start | bytes 49156

commit v2 on v1

--- a/solution.py
+++ b/solution.py
@@ -31,50 +31,84 @@
 NN = ((1,), (0,))
 
 
-def attend(nb, us, pair, qb, db, kvb, kT, table, acc, dqb):
+STRIP = 64
+FOLD = STRIP // 8
+
+
+def attend(nb, us, first, qb, db, kvb, kT, table, acc, dqb, score, dprob, low_p, low_ds):
     span = nb * 2 * TOK
-    cols = [pl.ds(pl.multiple_of(pair * 2 * WIDTH + g * WIDTH, WIDTH), WIDTH) for g in range(2)]
-    rows_q = jnp.concatenate([qb[us, h, :, cols[g]] for g in range(2) for h in range(2)], axis=0)
-    rows_d = jnp.concatenate([db[us, h, :, cols[g]] for g in range(2) for h in range(2)], axis=0)
     n_rows = 4 * TOK
+    strips = [slice(i, i + STRIP) for i in range(0, span, STRIP)]
     key = kvb[us, 0:nb, :, 0].reshape(span, WIDTH)
     val = kvb[us, 0:nb, :, 1].reshape(span, WIDTH)
-    score = dot(key, rows_q, NT)
-    kpos = lax.broadcasted_iota(jnp.int32, (2 * TOK, n_rows), 0)
-    rpos = lax.broadcasted_iota(jnp.int32, (2 * TOK, n_rows), 1) & (2 * TOK - 1)
-    diagonal = jnp.where(kpos <= rpos, score[: 2 * TOK], -jnp.inf)
-    score = diagonal if nb == 1 else jnp.concatenate([diagonal, score[2 * TOK :]], axis=0)
-    dprob = dot(val, rows_d, NT)
-    top = jnp.max(score, axis=0, keepdims=True)
-    weight = jnp.exp2((score - top) * EXP2_SCALE)
-    total = jnp.sum(weight, axis=0, keepdims=True)
-    mixed = jnp.sum(weight * dprob, axis=0, keepdims=True)
-    inverse = 1.0 / total
-    delta = mixed * inverse
-    prob = weight * inverse
-    ds = (prob * (dprob - delta)).astype(BF16)
-    acc[1, :span] += dot(prob.astype(BF16), rows_d, NN)
-    acc[0, :span] += dot(ds, rows_q, NN)
-    dqT = dot(kT[:, :span], ds, NN)
-    cos = jnp.concatenate([table[0], table[0]], axis=1)
-    sin = jnp.concatenate([table[1], table[1]], axis=1)
-    front = dqT[: WIDTH // 2] * SCORE_SCALE
-    back = dqT[WIDTH // 2 :] * SCORE_SCALE
-    turned = jnp.concatenate([front * cos + back * sin, back * cos - front * sin], axis=0)
-    dq = turned.T.astype(BF16)
-    for g in range(2):
-        for h in range(2):
-            at = (g * 2 + h) * TOK
-            dqb[us, h, :, cols[g]] = dq[at : at + TOK]
+    fold = (FOLD, 8, n_rows)
+
+    def columns(pair, g):
+        return pl.ds(pl.multiple_of((first + pair) * 2 * WIDTH + g * WIDTH, WIDTH), WIDTH)
+
+    def rows(ref, pair):
+        return jnp.concatenate([ref[us, h, :, columns(pair, g)] for g in range(2) for h in range(2)], axis=0)
+
+    def products(pair):
+        score[pair, :span] = dot(key, rows(qb, pair), NT)
+        dprob[pair, :span] = dot(val, rows(db, pair), NT)
+
+    def softmax(pair):
+        top = jnp.full((8, n_rows), -jnp.inf, F32)
+        for at in strips:
+            s = score[pair, at]
+            if at.start < 2 * TOK:
+                kpos = lax.broadcasted_iota(jnp.int32, (STRIP, n_rows), 0) + at.start
+                rpos = lax.broadcasted_iota(jnp.int32, (STRIP, n_rows), 1) & (2 * TOK - 1)
+                s = jnp.where(kpos <= rpos, s, -jnp.inf)
+                score[pair, at] = s
+            top = jnp.maximum(top, jnp.max(s.reshape(fold), axis=0))
+        top = jnp.max(top, axis=0, keepdims=True)
+        total = jnp.zeros((8, n_rows), F32)
+        mixed = jnp.zeros((8, n_rows), F32)
+        for at in strips:
+            weight = jnp.exp2((score[pair, at] - top) * EXP2_SCALE)
+            score[pair, at] = weight
+            total = total + jnp.sum(weight.reshape(fold), axis=0)
+            mixed = mixed + jnp.sum((weight * dprob[pair, at]).reshape(fold), axis=0)
+        inverse = 1.0 / jnp.sum(total, axis=0, keepdims=True)
+        delta = jnp.sum(mixed, axis=0, keepdims=True) * inverse
+        for at in strips:
+            prob = score[pair, at] * inverse
+            low_p[pair, at] = prob.astype(BF16)
+            low_ds[pair, at] = (prob * (dprob[pair, at] - delta)).astype(BF16)
+
+    def gradients(pair):
+        acc[1, :span] += dot(low_p[pair, :span], rows(db, pair), NN)
+        acc[0, :span] += dot(low_ds[pair, :span], rows(qb, pair), NN)
+        dqT = dot(kT[:, :span], low_ds[pair, :span], NN)
+        cos = jnp.concatenate([table[0], table[0]], axis=1)
+        sin = jnp.concatenate([table[1], table[1]], axis=1)
+        front = dqT[: WIDTH // 2] * SCORE_SCALE
+        back = dqT[WIDTH // 2 :] * SCORE_SCALE
+        turned = jnp.concatenate([front * cos + back * sin, back * cos - front * sin], axis=0)
+        dq = turned.T.astype(BF16)
+        for g in range(2):
+            for h in range(2):
+                at = (g * 2 + h) * TOK
+                dqb[us, h, :, columns(pair, g)] = dq[at : at + TOK]
+
+    products(0)
+    products(1)
+    softmax(0)
+    gradients(0)
+    softmax(1)
+    gradients(1)
 
 
 def main_kernel(
     n, ndp,
     flags, q_hbm, d_hbm, k_in, v_in, sq, sv, tables,
-    qg, kg, vg, qa, va,
+    qgs, kvg, gat,
     q, d, table, qsend, dsend, kv,
-    qb, db, kvb, st, stb, kT, acc, psend, rbuf, dqb, qgs, own,
-    vpart, msg, zr, zsum, dr, res, gat,
+    qb, db, kvb, st, stb, kT, acc, psend, rbuf, dqb, own,
+    vpart, msg, zr, zsum, dr, res,
+    score, dprob, low_p, low_ds,
     loads, kvs, kvr, qs, qr, ss, sr, ps, pr, dqs, dqr,
     zs_s, zr_s, ds_s, dr_s, as_s, ar_s,
 ):
@@ -224,9 +258,9 @@
         for count in range(1, GROUP_CHIPS + 1):
             @pl.when(nb == count)
             def _(count=count):
-                @pl.loop(0, PER_GROUP // 2)
-                def _(pair):
-                    attend(count, us, pair, qb, db, kvb, kT, table, acc, dqb)
+                @pl.loop(0, PER_GROUP // 2, step=2)
+                def _(first):
+                    attend(count, us, first, qb, db, kvb, kT, table, acc, dqb, score, dprob, low_p, low_ds)
 
         near_dq(us).start()
 
@@ -324,15 +358,9 @@
 
     gat[me] = res[...]
 
-    def spread(h):
-        return [share(h, s // 2, s % 2) for s in range(KV_HEADS)]
-
     @pl.loop(0, 2)
     def _(us):
         copy(dqb.at[us, other], qgs.at[2 * other + us], dqs.at[us], dqr.at[us], (dpi, sib)).wait_recv()
-
-    for h in range(KV_HEADS):
-        qg[:, h * SPAN : (h + 1) * SPAN] = pick([qgs[s] for s in range(KV_HEADS)], spread(h))
 
     @pl.loop(0, 2)
     def _(us):
@@ -342,24 +370,16 @@
     sin = jnp.where(c == 0, table[1, :, :TOK], table[1, :, TOK:]).T
     cos = jnp.concatenate([cos, cos], axis=1)
     sin = jnp.concatenate([sin, -sin], axis=1)
-    for h in range(KV_HEADS):
-        at = slice(h * WIDTH, (h + 1) * WIDTH)
-        dk = pick([own[s % 2, s // 2, 0] for s in range(KV_HEADS)], spread(h)) * SCORE_SCALE
-        kg[:, at] = (dk * cos + pltpu.roll(dk, WIDTH // 2, 1) * sin).astype(BF16)
-        vg[:, at] = pick([own[s % 2, s // 2, 1] for s in range(KV_HEADS)], spread(h)).astype(BF16)
+    for cc in range(2):
+        for us in range(2):
+            dk = own[us, cc, 0] * SCORE_SCALE
+            kvg[2 * cc + us, 0] = (dk * cos + pltpu.roll(dk, WIDTH // 2, 1) * sin).astype(BF16)
+            kvg[2 * cc + us, 1] = own[us, cc, 1].astype(BF16)
 
     @pl.loop(1, n)
     def _(o):
         k = (me + o) % n
         copy(res, gat.at[k], as_s.at[o], ar_s.at[k], (dpi, sib)).wait_recv()
-
-    for h in range(KV_HEADS):
-        for j in range(nz // 2):
-            at = h * SPAN + j * wide
-            held = [gat[2 * (s % 2 * (nz // 2) + j) + s // 2, :, :wide] for s in range(KV_HEADS)]
-            qa[:, at : at + wide] = pick(held, spread(h))
-        held = [gat[s // 2, :, wide + s % 2 * WIDTH : wide + (s % 2 + 1) * WIDTH] for s in range(KV_HEADS)]
-        va[:, h * WIDTH : (h + 1) * WIDTH] = pick(held, spread(h))
 
     @pl.loop(0, 2)
     def _(us):
@@ -408,17 +428,14 @@
     smem = pl.BlockSpec(memory_space=pltpu.SMEM)
     away = pl.BlockSpec(memory_space=pl.ANY)
     dma = pltpu.SemaphoreType.DMA
-    hw = KV_HEADS * WIDTH
     return pl.pallas_call(
         functools.partial(main_kernel, n, ndp),
         in_specs=[smem, away, away, vmem, vmem, vmem, vmem, away],
-        out_specs=[vmem] * 5,
+        out_specs=[vmem] * 3,
         out_shape=[
-            jax.ShapeDtypeStruct((TOK, KV_HEADS * SPAN), BF16),
-            jax.ShapeDtypeStruct((TOK, hw), BF16),
-            jax.ShapeDtypeStruct((TOK, hw), BF16),
-            jax.ShapeDtypeStruct((8, KV_HEADS * SPAN), F32),
-            jax.ShapeDtypeStruct((8, hw), F32),
+            jax.ShapeDtypeStruct((KV_HEADS, TOK, SPAN), BF16),
+            jax.ShapeDtypeStruct((KV_HEADS, 2, TOK, WIDTH), BF16),
+            jax.ShapeDtypeStruct((n, 8, line), F32),
         ],
         scratch_shapes=[
             pltpu.VMEM((TOK, KV_HEADS * SPAN), BF16),
@@ -437,7 +454,6 @@
             pltpu.VMEM((2, GROUP_CHIPS, 2, 2, TOK, WIDTH), BF16),
             pltpu.VMEM((2, GROUP_CHIPS, 2, 2, TOK, WIDTH), BF16),
             pltpu.VMEM((2, 2, TOK, SPAN), BF16),
-            pltpu.VMEM((KV_HEADS, TOK, SPAN), BF16),
             pltpu.VMEM((2, 2, 2, TOK, WIDTH), F32),
             pltpu.VMEM((2, 16, WIDTH), F32),
             pltpu.VMEM((nz, 8, line), F32),
@@ -445,7 +461,10 @@
             pltpu.VMEM((8, line), F32),
             pltpu.VMEM((ndp, 8, line), F32),
             pltpu.VMEM((8, line), F32),
-            pltpu.VMEM((n, 8, line), F32),
+            pltpu.VMEM((2, GROUP_CHIPS * 2 * TOK, 4 * TOK), F32),
+            pltpu.VMEM((2, GROUP_CHIPS * 2 * TOK, 4 * TOK), F32),
+            pltpu.VMEM((2, GROUP_CHIPS * 2 * TOK, 4 * TOK), BF16),
+            pltpu.VMEM((2, GROUP_CHIPS * 2 * TOK, 4 * TOK), BF16),
             dma((3,)),
             dma((2, GROUP_CHIPS, 2)), dma((2, GROUP_CHIPS, 2)),
             dma((2, 2)), dma((2, 2)),
@@ -457,10 +476,45 @@
             dma((n,)), dma((n,)),
         ],
         compiler_params=pltpu.CompilerParams(
-            collective_id=0, has_side_effects=True, vmem_limit_bytes=56 * 1024 * 1024
+            collective_id=0, has_side_effects=True, vmem_limit_bytes=48 * 1024 * 1024
         ),
         name="attention_backward",
     )(*operands)
+
+
+def restore_kernel(n, flags, qgs, kvg, gat, qg, kg, vg, qa, va):
+    nz = n // 2
+    wide = 2 * SPAN // nz
+    for h in range(KV_HEADS):
+        us = flags[h]
+        cc = sum((jnp.where(flags[j] == us, 1, 0) for j in range(h)), jnp.int32(0))
+        qg[:, h * SPAN : (h + 1) * SPAN] = qgs[2 * cc + us]
+        kg[:, h * WIDTH : (h + 1) * WIDTH] = kvg[2 * cc + us, 0]
+        vg[:, h * WIDTH : (h + 1) * WIDTH] = kvg[2 * cc + us, 1]
+        for j in range(nz // 2):
+            at = h * SPAN + j * wide
+            qa[:, at : at + wide] = gat[2 * (us * (nz // 2) + j) + cc, :, :wide]
+        at = pl.ds(pl.multiple_of(wide + us * WIDTH, WIDTH), WIDTH)
+        va[:, h * WIDTH : (h + 1) * WIDTH] = gat[cc, :, at]
+
+
+def restore(n, flags, *operands):
+    vmem = pl.BlockSpec(memory_space=pltpu.VMEM)
+    hw = KV_HEADS * WIDTH
+    return pl.pallas_call(
+        functools.partial(restore_kernel, n),
+        in_specs=[pl.BlockSpec(memory_space=pltpu.SMEM)] + [vmem] * 3,
+        out_specs=[vmem] * 5,
+        out_shape=[
+            jax.ShapeDtypeStruct((TOK, KV_HEADS * SPAN), BF16),
+            jax.ShapeDtypeStruct((TOK, hw), BF16),
+            jax.ShapeDtypeStruct((TOK, hw), BF16),
+            jax.ShapeDtypeStruct((8, KV_HEADS * SPAN), F32),
+            jax.ShapeDtypeStruct((8, hw), F32),
+        ],
+        compiler_params=pltpu.CompilerParams(vmem_limit_bytes=16 * 1024 * 1024),
+        name="restore_heads",
+    )(flags, *operands)
 
 
 def position_tables(n):
@@ -472,9 +526,10 @@
 
 def local(n, ndp, query, keys, values, out_grad, query_state, value_state, flags):
     tables = jnp.asarray(position_tables(n))
-    qg, kg, vg, qa, va = main_call(
+    places = main_call(
         n, ndp, flags, query[0], out_grad[0], keys[0], values[0], query_state[0].T, value_state[0].T, tables
     )
+    qg, kg, vg, qa, va = restore(n, flags, *places)
     return qg[None], kg[None], vg[None], qa, va
 
 

time: 60.5 us -> 60.9 us (level)
    pallas_call x1, Pallas kernels: 54.1 us -> 52.3 us  [main_call(): pl.pallas_call(functools.partial(main_kernel, n, ndp), in_specs=[smem, aw...]
    pallas_call x0 -> x1, Pallas kernels: none -> 1.71 us  [restore(): pl.pallas_call(functools.partial(restore_kernel, n), in_specs=[pl.BlockSp...]
    unnamed x13 -> x16, local copies, waits for them, and re-layouts: 5.55 us -> 5.97 us
where the time goes in v2:
time: 60.9 us; the launch traced here: 60.6 us
  Pallas kernels  54 us (89%)
  local copies, waits for them, and re-layouts  5.97 us (10%)
  between operations  0.67 us (1%)
    pallas_call x1, Pallas kernels, main_call(): pl.pallas_call(functools.partial(main_kernel, n, ndp), in_specs=[smem, aw...  52.3 us
    unnamed x16, local copies, waits for them, and re-layouts  5.97 us
    pallas_call x1, Pallas kernels, restore(): pl.pallas_call(functools.partial(restore_kernel, n), in_specs=[pl.BlockSp...  1.71 us

profile of v2, /device:TPU:0, one launch (start us, length us, event | category | flops | bytes accessed | tf_op | source)
XLA Modules:
  0.0 60.6 jit_solution(8508430379057328931)
XLA Ops:
  0.6 0.0 copy-start.6
  0.6 0.0 copy-start.5
  0.7 0.0 copy-start.7
  0.7 0.7 %copy-done.6 = bf16[1,128,8]{1,2,0:T(8,128)(2,1)S(1)} copy-done((bf16[1,128,8]{1,2,0:T(8,128)(2,1)S(1)}, bf16[1,128,8]{1,2,0:T(8,128)(2,1)}, u32[]{:S(2)}) %copy-start.6) | copy-done | bytes 2072
  1.3 0.0 copy-done.5
  1.3 0.0 copy-done.7
  1.3 0.0 copy-start
  1.3 1.2 %copy-done = bf16[1,128,4096]{2,1,0:T(8,128)(2,1)S(1)} copy-done((bf16[1,128,4096]{2,1,0:T(8,128)(2,1)S(1)}, bf16[1,128,4096]{2,1,0:T(8,128)(2,1)}, u32[]{:S(2)}) %copy-start) | copy-done | bytes 1048600
  2.6 0.0 copy-start.1
  2.6 1.2 %copy-done.1 = bf16[1,128,4096]{2,1,0:T(8,128)(2,1)S(1)} copy-done((bf16[1,128,4096]{2,1,0:T(8,128)(2,1)S(1)}, bf16[1,128,4096]{2,1,0:T(8,128)(2,1)}, u32[]{:S(2)}) %copy-start.1) | copy-done | bytes 1048600
  3.8 0.0 copy-start.2
  3.8 1.0 %copy-done.2 = f32[4,2,64,256]{3,2,1,0:T(8,128)S(1)} copy-done((f32[4,2,64,256]{3,2,1,0:T(8,128)S(1)}, f32[4,2,64,256]{3,2,1,0:T(8,128)}, u32[]{:S(2)}) %copy-start.2) | copy-done | bytes 524312
  4.8 0.0 copy-start.3
  4.8 0.9 %copy-done.3 = bf16[1,128,512]{2,1,0:T(8,128)(2,1)S(1)} copy-done((bf16[1,128,512]{2,1,0:T(8,128)(2,1)S(1)}, bf16[1,128,512]{2,1,0:T(8,128)(2,1)}, u32[]{:S(2)}) %copy-start.3) | copy-done | bytes 131096
  5.7 0.0 copy-start.4
  5.7 0.9 %copy-done.4 = bf16[1,128,512]{2,1,0:T(8,128)(2,1)S(1)} copy-done((bf16[1,128,512]{2,1,0:T(8,128)(2,1)S(1)}, bf16[1,128,512]{2,1,0:T(8,128)(2,1)}, u32[]{:S(2)}) %copy-start.4) | copy-done | bytes 131096
  6.6 52.3 %attention_backward.1 = (bf16[4,128,1024]{2,1,0:T(8,128)(2,1)S(1)}, bf16[4,2,128,128]{3,2,1,0:T(8,128)(2,1)S(1)}, f32[8,8,768]{2,1,0:T(8,128)S(1)}) custom-call(s32[4]{0:T(128)S(1)} %copy-done.7, bf16[128,4096]{1,0:T(8,128)(2,1)S(1)} %bitcast.13, bf16[128,4096]{1,0:T(8,128)(2,1)S(1)} %bitcast.14, bf16[128,512]{1,0:T(8,128)(2,1)S(1)} %bitcast.15, ...), custom_call_target="tpu_custom_call" | custom-call | tf_op jit(solution)/shard_map/attention_backward/pallas_call | solution.py:431
  58.9 1.7 %restore_heads.1 = (bf16[128,4096]{1,0:T(8,128)(2,1)}, bf16[128,512]{1,0:T(8,128)(2,1)}, bf16[128,512]{1,0:T(8,128)(2,1)}, f32[8,4096]{1,0:T(8,128)}, f32[8,512]{1,0:T(8,128)}) custom-call(s32[4]{0:T(128)S(1)} %copy-done.7, bf16[4,128,1024]{2,1,0:T(8,128)(2,1)S(1)} %get-tuple-element.13.qgs, bf16[4,2,128,128]{3,2,1,0:T(8,128)(2,1)S(1)} %get-tuple-element.14.kvg, ...), custom_call_target="tpu_custom_call" | custom-call | tf_op jit(solution)/shard_map/restore_heads/pallas_call | solution.py:504
Async XLA Ops:
  0.6 0.7 %copy-start.6 = (bf16[1,128,8]{1,2,0:T(8,128)(2,1)S(1)}, bf16[1,128,8]{1,2,0:T(8,128)(2,1)}, u32[]{:S(2)}) copy-start(bf16[1,128,8]{1,2,0:T(8,128)(2,1)} %param.13) | copy-start | bytes 6148
  0.6 0.7 %copy-start.5 = (bf16[1,128,8]{1,2,0:T(8,128)(2,1)S(1)}, bf16[1,128,8]{1,2,0:T(8,128)(2,1)}, u32[]{:S(2)}) copy-start(bf16[1,128,8]{1,2,0:T(8,128)(2,1)} %param.12) | copy-start | bytes 6148
  0.7 0.7 %copy-start.7 = (s32[4]{0:T(128)S(1)}, s32[4]{0:T(128)}, u32[]{:S(2)}) copy-start(s32[4]{0:T(128)} %flags.3) | copy-start | bytes 52
  1.3 1.2 %copy-start = (bf16[1,128,4096]{2,1,0:T(8,128)(2,1)S(1)}, bf16[1,128,4096]{2,1,0:T(8,128)(2,1)}, u32[]{:S(2)}) copy-start(bf16[1,128,4096]{2,1,0:T(8,128)(2,1)} %param.8) | copy-start | bytes 3145732
  2.6 1.2 %copy-start.1 = (bf16[1,128,4096]{2,1,0:T(8,128)(2,1)S(1)}, bf16[1,128,4096]{2,1,0:T(8,128)(2,1)}, u32[]{:S(2)}) copy-start(bf16[1,128,4096]{2,1,0:T(8,128)(2,1)} %param.11) | copy-start | bytes 3145732
  3.8 1.0 %copy-start.2 = (f32[4,2,64,256]{3,2,1,0:T(8,128)S(1)}, f32[4,2,64,256]{3,2,1,0:T(8,128)}, u32[]{:S(2)}) copy-start(f32[4,2,64,256]{3,2,1,0:T(8,128)} %constant.2.clone.tables) | copy-start | bytes 1572868
  4.8 0.9 %copy-start.3 = (bf16[1,128,512]{2,1,0:T(8,128)(2,1)S(1)}, bf16[1,128,512]{2,1,0:T(8,128)(2,1)}, u32[]{:S(2)}) copy-start(bf16[1,128,512]{2,1,0:T(8,128)(2,1)} %param.9) | copy-start | bytes 393220
  5.7 0.9 %copy-start.4 = (bf16[1,128,512]{2,1,0:T(8,128)(2,1)S(1)}, bf16[1,128,512]{2,1,0:T(8,128)(2,1)}, u32[]{:S(2)}) copy-start(bf16[1,128,512]{2,1,0:T(8,128)(2,1)} %param.10) | copy-start | bytes 393220

commit v3 on v2

--- a/solution.py
+++ b/solution.py
@@ -32,73 +32,17 @@
 
 
 STRIP = 64
-FOLD = STRIP // 8
-
-
-def attend(nb, us, first, qb, db, kvb, kT, table, acc, dqb, score, dprob, low_p, low_ds):
-    span = nb * 2 * TOK
-    n_rows = 4 * TOK
-    strips = [slice(i, i + STRIP) for i in range(0, span, STRIP)]
-    key = kvb[us, 0:nb, :, 0].reshape(span, WIDTH)
-    val = kvb[us, 0:nb, :, 1].reshape(span, WIDTH)
-    fold = (FOLD, 8, n_rows)
-
-    def columns(pair, g):
-        return pl.ds(pl.multiple_of((first + pair) * 2 * WIDTH + g * WIDTH, WIDTH), WIDTH)
-
-    def rows(ref, pair):
-        return jnp.concatenate([ref[us, h, :, columns(pair, g)] for g in range(2) for h in range(2)], axis=0)
-
-    def products(pair):
-        score[pair, :span] = dot(key, rows(qb, pair), NT)
-        dprob[pair, :span] = dot(val, rows(db, pair), NT)
-
-    def softmax(pair):
-        top = jnp.full((8, n_rows), -jnp.inf, F32)
-        for at in strips:
-            s = score[pair, at]
-            if at.start < 2 * TOK:
-                kpos = lax.broadcasted_iota(jnp.int32, (STRIP, n_rows), 0) + at.start
-                rpos = lax.broadcasted_iota(jnp.int32, (STRIP, n_rows), 1) & (2 * TOK - 1)
-                s = jnp.where(kpos <= rpos, s, -jnp.inf)
-                score[pair, at] = s
-            top = jnp.maximum(top, jnp.max(s.reshape(fold), axis=0))
-        top = jnp.max(top, axis=0, keepdims=True)
-        total = jnp.zeros((8, n_rows), F32)
-        mixed = jnp.zeros((8, n_rows), F32)
-        for at in strips:
-            weight = jnp.exp2((score[pair, at] - top) * EXP2_SCALE)
-            score[pair, at] = weight
-            total = total + jnp.sum(weight.reshape(fold), axis=0)
-            mixed = mixed + jnp.sum((weight * dprob[pair, at]).reshape(fold), axis=0)
-        inverse = 1.0 / jnp.sum(total, axis=0, keepdims=True)
-        delta = jnp.sum(mixed, axis=0, keepdims=True) * inverse
-        for at in strips:
-            prob = score[pair, at] * inverse
-            low_p[pair, at] = prob.astype(BF16)
-            low_ds[pair, at] = (prob * (dprob[pair, at] - delta)).astype(BF16)
-
-    def gradients(pair):
-        acc[1, :span] += dot(low_p[pair, :span], rows(db, pair), NN)
-        acc[0, :span] += dot(low_ds[pair, :span], rows(qb, pair), NN)
-        dqT = dot(kT[:, :span], low_ds[pair, :span], NN)
-        cos = jnp.concatenate([table[0], table[0]], axis=1)
-        sin = jnp.concatenate([table[1], table[1]], axis=1)
-        front = dqT[: WIDTH // 2] * SCORE_SCALE
-        back = dqT[WIDTH // 2 :] * SCORE_SCALE
-        turned = jnp.concatenate([front * cos + back * sin, back * cos - front * sin], axis=0)
-        dq = turned.T.astype(BF16)
-        for g in range(2):
-            for h in range(2):
-                at = (g * 2 + h) * TOK
-                dqb[us, h, :, columns(pair, g)] = dq[at : at + TOK]
-
-    products(0)
-    products(1)
-    softmax(0)
-    gradients(0)
-    softmax(1)
-    gradients(1)
+BLOCK = 2 * TOK
+PAIRS = PER_GROUP // 2
+ROWS = 4 * TOK
+
+
+def fold(x):
+    return x.reshape(x.shape[0] // 8, 8, x.shape[1])
+
+
+def spread(x):
+    return jnp.broadcast_to(x, (8, x.shape[1]))
 
 
 def main_kernel(
@@ -106,9 +50,9 @@
     flags, q_hbm, d_hbm, k_in, v_in, sq, sv, tables,
     qgs, kvg, gat,
     q, d, table, qsend, dsend, kv,
-    qb, db, kvb, st, stb, kT, acc, psend, rbuf, dqb, own,
+    qb, db, kvb, st, stb, kT, psend, rbuf, dqb, own,
     vpart, msg, zr, zsum, dr, res,
-    score, dprob, low_p, low_ds,
+    score, dprob, low_p, low_ds, dqT, top, total, mixed,
     loads, kvs, kvr, qs, qr, ss, sr, ps, pr, dqs, dqr,
     zs_s, zr_s, ds_s, dr_s, as_s, ar_s,
 ):
@@ -242,34 +186,78 @@
         copy(kv.at[0], kvb.at[us, 0, other], kvs.at[us, 0, other], kvr.at[us, 0, other], (dpi, sib)).wait_recv()
         near_rows(us, 0).wait_recv()
         near_rows(us, 1).wait_recv()
-
-        @pl.loop(1, nb)
-        def _(t):
-            for h in range(2):
-                copy(kv.at[0], kvb.at[us, t, h], kvs.at[us, t, h], kvr.at[us, t, h], (dpi, sib)).wait_recv()
+        for pair in range(PAIRS):
+            top[pair] = jnp.full((8, ROWS), -jnp.inf, F32)
+            total[pair] = jnp.zeros((8, ROWS), F32)
+            mixed[pair] = jnp.zeros((8, ROWS), F32)
+
+        def rows(ref, pair):
+            heads = [slice((2 * pair + g) * WIDTH, (2 * pair + g + 1) * WIDTH) for g in range(2)]
+            return jnp.concatenate([ref[us, h, :, heads[g]] for g in range(2) for h in range(2)], axis=0)
 
         @pl.loop(0, nb)
         def _(t):
-            at = pl.ds(pl.multiple_of(t * 2 * TOK, 2 * TOK), 2 * TOK)
-            kT[:, at] = kvb[us, t, :, 0].reshape(2 * TOK, WIDTH).astype(F32).T.astype(BF16)
-            acc[0, at] = jnp.zeros((2 * TOK, WIDTH), F32)
-            acc[1, at] = jnp.zeros((2 * TOK, WIDTH), F32)
-
-        for count in range(1, GROUP_CHIPS + 1):
-            @pl.when(nb == count)
-            def _(count=count):
-                @pl.loop(0, PER_GROUP // 2, step=2)
-                def _(first):
-                    attend(count, us, first, qb, db, kvb, kT, table, acc, dqb, score, dprob, low_p, low_ds)
-
-        near_dq(us).start()
+            @pl.when(t > 0)
+            def _():
+                for h in range(2):
+                    copy(kv.at[0], kvb.at[us, t, h], kvs.at[us, t, h], kvr.at[us, t, h], (dpi, sib)).wait_recv()
+
+            key = kvb[us, t, :, 0].reshape(BLOCK, WIDTH)
+            val = kvb[us, t, :, 1].reshape(BLOCK, WIDTH)
+            at = pl.ds(pl.multiple_of(t * BLOCK, BLOCK), BLOCK)
+            kT[:, at] = key.astype(F32).T.astype(BF16)
+            kpos = lax.broadcasted_iota(jnp.int32, (BLOCK, ROWS), 0)
+            rpos = lax.broadcasted_iota(jnp.int32, (BLOCK, ROWS), 1) & (BLOCK - 1)
+            seen = kpos <= rpos + t * BLOCK
+            for pair in range(PAIRS):
+                s = jnp.where(seen, dot(key, rows(qb, pair), NT), -jnp.inf)
+                score[pair, t] = s
+                top[pair] = jnp.maximum(top[pair], jnp.max(fold(s), axis=0))
+                dprob[pair, t] = dot(val, rows(db, pair), NT)
+
+        for pair in range(PAIRS):
+            top[pair] = spread(jnp.max(top[pair], axis=0, keepdims=True))
 
         @pl.loop(0, nb)
         def _(t):
+            for pair in range(PAIRS):
+                high = top[pair]
+                sum_w = total[pair]
+                sum_m = mixed[pair]
+                for i in range(0, BLOCK, STRIP):
+                    at = slice(i, i + STRIP)
+                    weight = jnp.exp2((fold(score[pair, t, at]) - high) * EXP2_SCALE)
+                    score[pair, t, at] = weight.reshape(STRIP, ROWS)
+                    sum_w = sum_w + jnp.sum(weight, axis=0)
+                    sum_m = sum_m + jnp.sum(weight * fold(dprob[pair, t, at]), axis=0)
+                total[pair] = sum_w
+                mixed[pair] = sum_m
+
+        for pair in range(PAIRS):
+            inverse = 1.0 / jnp.sum(total[pair], axis=0, keepdims=True)
+            delta = jnp.sum(mixed[pair], axis=0, keepdims=True) * inverse
+            total[pair] = spread(inverse)
+            mixed[pair] = spread(delta)
+
+        @pl.loop(0, nb)
+        def _(back):
+            t = nb - 1 - back
+            dk = jnp.zeros((BLOCK, WIDTH), F32)
+            dv = jnp.zeros((BLOCK, WIDTH), F32)
+            for pair in range(PAIRS):
+                inverse = total[pair]
+                delta = mixed[pair]
+                for i in range(0, BLOCK, STRIP):
+                    at = slice(i, i + STRIP)
+                    prob = fold(score[pair, t, at]) * inverse
+                    ds = prob * (fold(dprob[pair, t, at]) - delta)
+                    low_p[pair, at] = prob.reshape(STRIP, ROWS).astype(BF16)
+                    low_ds[pair, t, at] = ds.reshape(STRIP, ROWS).astype(BF16)
+                dv = dv + dot(low_p[pair], rows(db, pair), NN)
+                dk = dk + dot(low_ds[pair, t], rows(qb, pair), NN)
             for h in range(2):
-                at = pl.ds(pl.multiple_of(t * 2 * TOK + h * TOK, TOK), TOK)
-                psend[us, t, h, 0] = acc[0, at].astype(BF16)
-                psend[us, t, h, 1] = acc[1, at].astype(BF16)
+                psend[us, t, h, 0] = dk[h * TOK : (h + 1) * TOK].astype(BF16)
+                psend[us, t, h, 1] = dv[h * TOK : (h + 1) * TOK].astype(BF16)
 
             @pl.when(t > 0)
             def _():
@@ -277,6 +265,26 @@
                 far_part(us, t, 1).start()
 
         near_part(us).start()
+
+        for count in range(1, GROUP_CHIPS + 1):
+            @pl.when(nb == count)
+            def _(count=count):
+                for pair in range(PAIRS):
+                    ds = low_ds[pair, 0:count].reshape(count * BLOCK, ROWS)
+                    dqT[pair] = dot(kT[:, : count * BLOCK], ds, NN)
+
+        cos = jnp.concatenate([table[0], table[0]], axis=1)
+        sin = jnp.concatenate([table[1], table[1]], axis=1)
+        for pair in range(PAIRS):
+            front = dqT[pair, : WIDTH // 2] * SCORE_SCALE
+            back = dqT[pair, WIDTH // 2 :] * SCORE_SCALE
+            turned = jnp.concatenate([front * cos + back * sin, back * cos - front * sin], axis=0)
+            dq = turned.T.astype(BF16)
+            for g in range(2):
+                for h in range(2):
+                    at = (g * 2 + h) * TOK
+                    dqb[us, h, :, (2 * pair + g) * WIDTH : (2 * pair + g + 1) * WIDTH] = dq[at : at + TOK]
+        near_dq(us).start()
 
         @pl.when(step == 0)
         def _():
@@ -450,7 +458,6 @@
             pltpu.VMEM((16, TOK), BF16),
             pltpu.VMEM((GROUP_CHIPS, 2, 16, TOK), BF16),
             pltpu.VMEM((WIDTH, GROUP_CHIPS * 2 * TOK), BF16),
-            pltpu.VMEM((2, GROUP_CHIPS * 2 * TOK, WIDTH), F32),
             pltpu.VMEM((2, GROUP_CHIPS, 2, 2, TOK, WIDTH), BF16),
             pltpu.VMEM((2, GROUP_CHIPS, 2, 2, TOK, WIDTH), BF16),
             pltpu.VMEM((2, 2, TOK, SPAN), BF16),
@@ -461,10 +468,14 @@
             pltpu.VMEM((8, line), F32),
             pltpu.VMEM((ndp, 8, line), F32),
             pltpu.VMEM((8, line), F32),
-            pltpu.VMEM((2, GROUP_CHIPS * 2 * TOK, 4 * TOK), F32),
-            pltpu.VMEM((2, GROUP_CHIPS * 2 * TOK, 4 * TOK), F32),
-            pltpu.VMEM((2, GROUP_CHIPS * 2 * TOK, 4 * TOK), BF16),
-            pltpu.VMEM((2, GROUP_CHIPS * 2 * TOK, 4 * TOK), BF16),
+            pltpu.VMEM((PAIRS, GROUP_CHIPS, BLOCK, ROWS), F32),
+            pltpu.VMEM((PAIRS, GROUP_CHIPS, BLOCK, ROWS), F32),
+            pltpu.VMEM((PAIRS, BLOCK, ROWS), BF16),
+            pltpu.VMEM((PAIRS, GROUP_CHIPS, BLOCK, ROWS), BF16),
+            pltpu.VMEM((PAIRS, WIDTH, ROWS), F32),
+            pltpu.VMEM((PAIRS, 8, ROWS), F32),
+            pltpu.VMEM((PAIRS, 8, ROWS), F32),
+            pltpu.VMEM((PAIRS, 8, ROWS), F32),
             dma((3,)),
             dma((2, GROUP_CHIPS, 2)), dma((2, GROUP_CHIPS, 2)),
             dma((2, 2)), dma((2, 2)),
@@ -476,7 +487,7 @@
             dma((n,)), dma((n,)),
         ],
         compiler_params=pltpu.CompilerParams(
-            collective_id=0, has_side_effects=True, vmem_limit_bytes=48 * 1024 * 1024
+            collective_id=0, has_side_effects=True, vmem_limit_bytes=56 * 1024 * 1024
         ),
         name="attention_backward",
     )(*operands)

time: 60.9 us -> 58.4 us (0.959)
  local copies, waits for them, and re-layouts: 5.97 us -> 3.75 us
    unnamed x16 -> x8, local copies, waits for them, and re-layouts: 5.97 us -> 3.75 us
where the time goes in v3:
time: 58.4 us; the launch traced here: 58.1 us
  Pallas kernels  53.7 us (92%)
  local copies, waits for them, and re-layouts  3.75 us (6%)
  between operations  0.65 us (1%)
    pallas_call x1, Pallas kernels, main_call(): pl.pallas_call(functools.partial(main_kernel, n, ndp), in_specs=[smem, aw...  52 us
    unnamed x8, local copies, waits for them, and re-layouts  3.75 us
    pallas_call x1, Pallas kernels, restore(): pl.pallas_call(functools.partial(restore_kernel, n), in_specs=[pl.BlockSp...  1.71 us

profile of v3, /device:TPU:0, one launch (start us, length us, event | category | flops | bytes accessed | tf_op | source)
XLA Modules:
  0.0 58.1 jit_solution(7874871840650698415)
XLA Ops:
  0.6 52.0 %attention_backward.1 = (bf16[4,128,1024]{2,1,0:T(8,128)(2,1)}, bf16[4,2,128,128]{3,2,1,0:T(8,128)(2,1)}, f32[8,8,768]{2,1,0:T(8,128)}) custom-call(s32[4]{0:T(128)} %flags.3, bf16[128,4096]{1,0:T(8,128)(2,1)} %bitcast.13, bf16[128,4096]{1,0:T(8,128)(2,1)} %bitcast.14, bf16[128,512]{1,0:T(8,128)(2,1)} %bitcast.15, bf16[128,512]{1,0:T(8,128)(2,1)} %bitcast.16, ...), custom_call_target="tpu_custom_call" | custom-call | tf_op jit(solution)/shard_map/attention_backward/pallas_call | solution.py:439
  52.7 0.0 copy-start.3
  52.7 0.6 %copy-done.3 = s32[4]{0:T(128)S(1)} copy-done((s32[4]{0:T(128)S(1)}, s32[4]{0:T(128)}, u32[]{:S(2)}) %copy-start.3) | copy-done | bytes 40
  53.3 0.0 copy-start
  53.3 1.2 %copy-done = bf16[4,128,1024]{2,1,0:T(8,128)(2,1)S(1)} copy-done((bf16[4,128,1024]{2,1,0:T(8,128)(2,1)S(1)}, bf16[4,128,1024]{2,1,0:T(8,128)(2,1)}, u32[]{:S(2)}) %copy-start) | copy-done | bytes 1048600
  54.5 0.0 copy-start.1
  54.5 0.9 %copy-done.1 = bf16[4,2,128,128]{3,2,1,0:T(8,128)(2,1)S(1)} copy-done((bf16[4,2,128,128]{3,2,1,0:T(8,128)(2,1)S(1)}, bf16[4,2,128,128]{3,2,1,0:T(8,128)(2,1)}, u32[]{:S(2)}) %copy-start.1) | copy-done | bytes 262168
  55.5 0.0 copy-start.2
  55.5 0.9 %copy-done.2 = f32[8,8,768]{2,1,0:T(8,128)S(1)} copy-done((f32[8,8,768]{2,1,0:T(8,128)S(1)}, f32[8,8,768]{2,1,0:T(8,128)}, u32[]{:S(2)}) %copy-start.2) | copy-done | bytes 196632
  56.4 1.7 %restore_heads.1 = (bf16[128,4096]{1,0:T(8,128)(2,1)}, bf16[128,512]{1,0:T(8,128)(2,1)}, bf16[128,512]{1,0:T(8,128)(2,1)}, f32[8,4096]{1,0:T(8,128)}, f32[8,512]{1,0:T(8,128)}) custom-call(s32[4]{0:T(128)S(1)} %copy-done.3, bf16[4,128,1024]{2,1,0:T(8,128)(2,1)S(1)} %copy-done, bf16[4,2,128,128]{3,2,1,0:T(8,128)(2,1)S(1)} %copy-done.1, f32[8,8,768]{2,1,0:T(8,128)S(1)} %copy-done.2), custom_call_target="tpu_custom_call" | custom-call | tf_op jit(solution)/shard_map/restore_heads/pallas_call | solution.py:515
Async XLA Ops:
  52.7 0.7 %copy-start.3 = (s32[4]{0:T(128)S(1)}, s32[4]{0:T(128)}, u32[]{:S(2)}) copy-start(s32[4]{0:T(128)} %flags.3) | copy-start | bytes 52
  53.3 1.2 %copy-start = (bf16[4,128,1024]{2,1,0:T(8,128)(2,1)S(1)}, bf16[4,128,1024]{2,1,0:T(8,128)(2,1)}, u32[]{:S(2)}) copy-start(bf16[4,128,1024]{2,1,0:T(8,128)(2,1)} %get-tuple-element.13.qgs) | copy-start | bytes 3145732
  54.5 0.9 %copy-start.1 = (bf16[4,2,128,128]{3,2,1,0:T(8,128)(2,1)S(1)}, bf16[4,2,128,128]{3,2,1,0:T(8,128)(2,1)}, u32[]{:S(2)}) copy-start(bf16[4,2,128,128]{3,2,1,0:T(8,128)(2,1)} %get-tuple-element.14.kvg) | copy-start | bytes 786436
  55.5 0.9 %copy-start.2 = (f32[8,8,768]{2,1,0:T(8,128)S(1)}, f32[8,8,768]{2,1,0:T(8,128)}, u32[]{:S(2)}) copy-start(f32[8,8,768]{2,1,0:T(8,128)} %get-tuple-element.15.gat) | copy-start | bytes 589828

commit v4 on v3

--- a/solution.py
+++ b/solution.py
@@ -48,13 +48,13 @@
 def main_kernel(
     n, ndp,
     flags, q_hbm, d_hbm, k_in, v_in, sq, sv, tables,
-    qgs, kvg, gat,
+    qgs, kvg, gat, vgat,
     q, d, table, qsend, dsend, kv,
     qb, db, kvb, st, stb, kT, psend, rbuf, dqb, own,
-    vpart, msg, zr, zsum, dr, res,
+    vpart, msg, zr, zsum, dr, res, vres,
     score, dprob, low_p, low_ds, dqT, top, total, mixed,
     loads, kvs, kvr, qs, qr, ss, sr, ps, pr, dqs, dqr,
-    zs_s, zr_s, ds_s, dr_s, as_s, ar_s,
+    zs_s, zr_s, ds_s, dr_s, as_s, ar_s, vr_s,
 ):
     nz = n // 2
     wide = 2 * SPAN // nz
@@ -118,15 +118,8 @@
         kv[s, 0] = gather(k_in, WIDTH, s // 2, s % 2)
         kv[s, 1] = gather(v_in, WIDTH, s // 2, s % 2)
     early = (z // 2) % 2
-    load_q.wait()
-    load_d.wait()
     for us in range(2):
-        qsend[us] = gather(q, SPAN, other, us)
-        dsend[us] = gather(d, SPAN, other, us)
-        qb[us, c] = gather(q, SPAN, c, us)
-        db[us, c] = gather(d, SPAN, c, us)
         kvb[us, 0, c] = kv[2 * c + us]
-    load_t.wait()
 
     pl.semaphore_wait(barrier, n - 1 + ndp - 1)
 
@@ -161,9 +154,6 @@
     @pl.loop(0, 2)
     def _(step):
         us = (step + early) % 2
-        near_kv(us).start()
-        near_rows(us, 0).start()
-        near_rows(us, 1).start()
 
         @pl.loop(1, GROUP_CHIPS)
         def _(t):
@@ -172,12 +162,29 @@
                 far_kv(us, t, 0).start()
                 far_kv(us, t, 1).start()
 
+        near_kv(us).start()
+
+    load_q.wait()
+    load_d.wait()
+
+    @pl.loop(0, 2)
+    def _(step):
+        us = (step + early) % 2
+        qsend[us] = gather(q, SPAN, other, us)
+        near_rows(us, 0).start()
+        dsend[us] = gather(d, SPAN, other, us)
+        near_rows(us, 1).start()
+        qb[us, c] = gather(q, SPAN, c, us)
+        db[us, c] = gather(d, SPAN, c, us)
+
     near_state().start()
 
     @pl.loop(1, GROUP_CHIPS)
     def _(t):
         far_state(t, 0).start()
         far_state(t, 1).start()
+
+    load_t.wait()
 
     @pl.loop(0, 2)
     def _(step):
@@ -353,18 +360,26 @@
         k = (dpi + o) % ndp
         copy(zsum, dr.at[k], ds_s.at[o], dr_s.at[k], (dpi, sib)).wait_recv()
 
-    res[...] = (
+    summed = (
         lax.fori_loop(0, ndp, lambda k, x: x + dr[k], jnp.zeros((8, wide + 2 * WIDTH), F32)) * ADAPTER_SCALE
     )
+    res[...] = summed[:, :wide]
+    vres[...] = summed[:, wide:]
 
     def to_ctx(o):
         return copy(res, gat.at[me], as_s.at[o], ar_s.at[me], (dpi, (me + o) % n))
 
+    def to_sib():
+        return copy(vres, vgat.at[c], as_s.at[0], vr_s, (dpi, sib))
+
+    to_sib().start()
+
     @pl.loop(1, n)
     def _(o):
         to_ctx(o).start()
 
     gat[me] = res[...]
+    vgat[c] = vres[...]
 
     @pl.loop(0, 2)
     def _(us):
@@ -388,6 +403,9 @@
     def _(o):
         k = (me + o) % n
         copy(res, gat.at[k], as_s.at[o], ar_s.at[k], (dpi, sib)).wait_recv()
+
+    copy(vres, vgat.at[other], as_s.at[0], vr_s, (dpi, sib)).wait_recv()
+    to_sib().wait_send()
 
     @pl.loop(0, 2)
     def _(us):
@@ -439,11 +457,12 @@
     return pl.pallas_call(
         functools.partial(main_kernel, n, ndp),
         in_specs=[smem, away, away, vmem, vmem, vmem, vmem, away],
-        out_specs=[vmem] * 3,
+        out_specs=[vmem] * 4,
         out_shape=[
             jax.ShapeDtypeStruct((KV_HEADS, TOK, SPAN), BF16),
             jax.ShapeDtypeStruct((KV_HEADS, 2, TOK, WIDTH), BF16),
-            jax.ShapeDtypeStruct((n, 8, line), F32),
+            jax.ShapeDtypeStruct((n, 8, line - 2 * WIDTH), F32),
+            jax.ShapeDtypeStruct((2, 8, 2 * WIDTH), F32),
         ],
         scratch_shapes=[
             pltpu.VMEM((TOK, KV_HEADS * SPAN), BF16),
@@ -467,7 +486,8 @@
             pltpu.VMEM((nz, 8, line), F32),
             pltpu.VMEM((8, line), F32),
             pltpu.VMEM((ndp, 8, line), F32),
-            pltpu.VMEM((8, line), F32),
+            pltpu.VMEM((8, line - 2 * WIDTH), F32),
+            pltpu.VMEM((8, 2 * WIDTH), F32),
             pltpu.VMEM((PAIRS, GROUP_CHIPS, BLOCK, ROWS), F32),
             pltpu.VMEM((PAIRS, GROUP_CHIPS, BLOCK, ROWS), F32),
             pltpu.VMEM((PAIRS, BLOCK, ROWS), BF16),
@@ -484,7 +504,7 @@
             dma((2,)), dma((2,)),
             dma((nz,)), dma((nz,)),
             dma((ndp,)), dma((ndp,)),
-            dma((n,)), dma((n,)),
+            dma((n,)), dma((n,)), dma,
         ],
         compiler_params=pltpu.CompilerParams(
             collective_id=0, has_side_effects=True, vmem_limit_bytes=56 * 1024 * 1024
@@ -493,7 +513,7 @@
     )(*operands)
 
 
-def restore_kernel(n, flags, qgs, kvg, gat, qg, kg, vg, qa, va):
+def restore_kernel(n, flags, qgs, kvg, gat, vgat, qg, kg, vg, qa, va):
     nz = n // 2
     wide = 2 * SPAN // nz
     for h in range(KV_HEADS):
@@ -504,9 +524,9 @@
         vg[:, h * WIDTH : (h + 1) * WIDTH] = kvg[2 * cc + us, 1]
         for j in range(nz // 2):
             at = h * SPAN + j * wide
-            qa[:, at : at + wide] = gat[2 * (us * (nz // 2) + j) + cc, :, :wide]
-        at = pl.ds(pl.multiple_of(wide + us * WIDTH, WIDTH), WIDTH)
-        va[:, h * WIDTH : (h + 1) * WIDTH] = gat[cc, :, at]
+            qa[:, at : at + wide] = gat[2 * (us * (nz // 2) + j) + cc]
+        at = pl.ds(pl.multiple_of(us * WIDTH, WIDTH), WIDTH)
+        va[:, h * WIDTH : (h + 1) * WIDTH] = vgat[cc, :, at]
 
 
 def restore(n, flags, *operands):
@@ -514,7 +534,7 @@
     hw = KV_HEADS * WIDTH
     return pl.pallas_call(
         functools.partial(restore_kernel, n),
-        in_specs=[pl.BlockSpec(memory_space=pltpu.SMEM)] + [vmem] * 3,
+        in_specs=[pl.BlockSpec(memory_space=pltpu.SMEM)] + [vmem] * 4,
         out_specs=[vmem] * 5,
         out_shape=[
             jax.ShapeDtypeStruct((TOK, KV_HEADS * SPAN), BF16),
@@ -523,7 +543,7 @@
             jax.ShapeDtypeStruct((8, KV_HEADS * SPAN), F32),
             jax.ShapeDtypeStruct((8, hw), F32),
         ],
-        compiler_params=pltpu.CompilerParams(vmem_limit_bytes=16 * 1024 * 1024),
+        compiler_params=pltpu.CompilerParams(vmem_limit_bytes=56 * 1024 * 1024),
         name="restore_heads",
     )(flags, *operands)
 

time: 58.4 us -> 54.8 us (0.938)
  local copies, waits for them, and re-layouts: 3.75 us -> 0 us
    unnamed x8 -> x0, local copies, waits for them, and re-layouts: 3.75 us -> none
    pallas_call x1, Pallas kernels: 1.71 us -> 2.5 us  [restore(): pl.pallas_call(functools.partial(restore_kernel, n), in_specs=[pl.BlockSp...]
where the time goes in v4:
time: 54.8 us; the launch traced here: 54.6 us
  Pallas kernels  54 us (99%)
  between operations  0.64 us (1%)
    pallas_call x1, Pallas kernels, main_call(): pl.pallas_call(functools.partial(main_kernel, n, ndp), in_specs=[smem, aw...  51.5 us
    pallas_call x1, Pallas kernels, restore(): pl.pallas_call(functools.partial(restore_kernel, n), in_specs=[pl.BlockSp...  2.5 us

profile of v4, /device:TPU:0, one launch (start us, length us, event | category | flops | bytes accessed | tf_op | source)
XLA Modules:
  0.0 54.6 jit_solution(736867004994421631)
XLA Ops:
  0.6 51.5 %attention_backward.1 = (bf16[4,128,1024]{2,1,0:T(8,128)(2,1)}, bf16[4,2,128,128]{3,2,1,0:T(8,128)(2,1)}, f32[8,8,512]{2,1,0:T(8,128)}, f32[2,8,256]{2,1,0:T(8,128)}) custom-call(s32[4]{0:T(128)} %flags.3, bf16[128,4096]{1,0:T(8,128)(2,1)} %bitcast.13, bf16[128,4096]{1,0:T(8,128)(2,1)} %bitcast.14, bf16[128,512]{1,0:T(8,128)(2,1)} %bitcast.15, ...), custom_call_target="tpu_custom_call" | custom-call | tf_op jit(solution)/shard_map/attention_backward/pallas_call | solution.py:457
  52.1 2.5 %restore_heads.1 = (bf16[128,4096]{1,0:T(8,128)(2,1)}, bf16[128,512]{1,0:T(8,128)(2,1)}, bf16[128,512]{1,0:T(8,128)(2,1)}, f32[8,4096]{1,0:T(8,128)}, f32[8,512]{1,0:T(8,128)}) custom-call(s32[4]{0:T(128)} %flags.3, bf16[4,128,1024]{2,1,0:T(8,128)(2,1)} %get-tuple-element.14.qgs, bf16[4,2,128,128]{3,2,1,0:T(8,128)(2,1)} %get-tuple-element.15.kvg, ...), custom_call_target="tpu_custom_call" | custom-call | tf_op jit(solution)/shard_map/restore_heads/pallas_call | solution.py:535

commit v5 on v4

--- a/solution.py
+++ b/solution.py
@@ -118,6 +118,7 @@
         kv[s, 0] = gather(k_in, WIDTH, s // 2, s % 2)
         kv[s, 1] = gather(v_in, WIDTH, s // 2, s % 2)
     early = (z // 2) % 2
+    large = 1 - early
     for us in range(2):
         kvb[us, 0, c] = kv[2 * c + us]
 
@@ -169,7 +170,7 @@
 
     @pl.loop(0, 2)
     def _(step):
-        us = (step + early) % 2
+        us = (step + large) % 2
         qsend[us] = gather(q, SPAN, other, us)
         near_rows(us, 0).start()
         dsend[us] = gather(d, SPAN, other, us)
@@ -188,7 +189,7 @@
 
     @pl.loop(0, 2)
     def _(step):
-        us = (step + early) % 2
+        us = (step + large) % 2
         nb = slot(us, z) + 1
         copy(kv.at[0], kvb.at[us, 0, other], kvs.at[us, 0, other], kvr.at[us, 0, other], (dpi, sib)).wait_recv()
         near_rows(us, 0).wait_recv()

time: 54.8 us -> 52.8 us (0.964)
  Pallas kernels: 54 us -> 52 us
    pallas_call x1, Pallas kernels: 51.5 us -> 49.5 us  [main_call(): pl.pallas_call(functools.partial(main_kernel, n, ndp), in_specs=[smem, aw...]
where the time goes in v5:
time: 52.8 us; the launch traced here: 52.6 us
  Pallas kernels  52 us (98%)
  between operations  0.64 us (1%)
    pallas_call x1, Pallas kernels, main_call(): pl.pallas_call(functools.partial(main_kernel, n, ndp), in_specs=[smem, aw...  49.5 us
    pallas_call x1, Pallas kernels, restore(): pl.pallas_call(functools.partial(restore_kernel, n), in_specs=[pl.BlockSp...  2.5 us

profile of v5, /device:TPU:0, one launch (start us, length us, event | category | flops | bytes accessed | tf_op | source)
XLA Modules:
  0.0 52.6 jit_solution(3969135180652126225)
XLA Ops:
  0.6 49.5 %attention_backward.1 = (bf16[4,128,1024]{2,1,0:T(8,128)(2,1)}, bf16[4,2,128,128]{3,2,1,0:T(8,128)(2,1)}, f32[8,8,512]{2,1,0:T(8,128)}, f32[2,8,256]{2,1,0:T(8,128)}) custom-call(s32[4]{0:T(128)} %flags.3, bf16[128,4096]{1,0:T(8,128)(2,1)} %bitcast.13, bf16[128,4096]{1,0:T(8,128)(2,1)} %bitcast.14, bf16[128,512]{1,0:T(8,128)(2,1)} %bitcast.15, ...), custom_call_target="tpu_custom_call" | custom-call | tf_op jit(solution)/shard_map/attention_backward/pallas_call | solution.py:458
  50.1 2.5 %restore_heads.1 = (bf16[128,4096]{1,0:T(8,128)(2,1)}, bf16[128,512]{1,0:T(8,128)(2,1)}, bf16[128,512]{1,0:T(8,128)(2,1)}, f32[8,4096]{1,0:T(8,128)}, f32[8,512]{1,0:T(8,128)}) custom-call(s32[4]{0:T(128)} %flags.3, bf16[4,128,1024]{2,1,0:T(8,128)(2,1)} %get-tuple-element.14.qgs, bf16[4,2,128,128]{3,2,1,0:T(8,128)(2,1)} %get-tuple-element.15.kvg, ...), custom_call_target="tpu_custom_call" | custom-call | tf_op jit(solution)/shard_map/restore_heads/pallas_call | solution.py:536
